TPU v7x, 32 devices: a whole 2x2x4 slice. The times are simulated.
32 devices in a mesh: wide: 8 (over z, y), narrow: 4 (over x, core).
Axes of the slice: x: 2, y: 2, z: 4, core: 2. Of those that a mesh axis runs over, the one named last changes fastest.
Arguments:
- points: bfloat16 [256, 256, 256], P('wide', 'narrow'), may hold values from -6 to 6
- targets: bfloat16 [256, 256, 256], P('wide', 'narrow'), may hold values from -6 to 6
- centroids: float32 [128, 256], P('wide'), may hold values from -3 to 3
- block_list: int32 [256], P('wide'), may hold values from 0 to 15
- lengths: int32 [256], P('wide'), may hold values from 1 to 256
- sources: int32 [256], P('wide'), may hold values from 0 to 255, as said below
Outputs:
- rotated: bfloat16 [256, 256, 256], P('wide', 'narrow')
Inputs may be any that keep to these rules, and one draw needn't show every extreme that they name: For every index w of wide and slot j below 2, sources[w * 32 + j] = u * 32 + j for some index u of wide, each such input block named exactly once; every other entry names its own position.
All inputs are finite; a program needn't handle non-finite values.
Results may differ from a plain program's by a relative error of at most 0.0051.
Values may be sent and summed in bfloat16 or wider, within the bound.
No kernel may reach another device: no remote copies, remote signals or barrier semaphores. Data moves between devices by JAX's collectives and lax.ppermute only.
A program may use at most 64 MiB of HBM per device.

v0:
```python
import functools

import jax
import jax.numpy as jnp
from jax import lax
from jax.experimental import pallas as pl
from jax.experimental.pallas import tpu as pltpu
from jax.sharding import PartitionSpec as P

MOVE = 2
ITERS = 5
CORES = 2
PIECES = 2
STORES = 8
VMEM_LIMIT = 14 * 1024 * 1024
LONG = 1 << 30
GROUP = 4
LEAD_FLOPS = 1350000000
PAIR_FLOPS = 1500000000

f32, bf16, i32 = jnp.float32, jnp.bfloat16, jnp.int32

SMEM = pl.BlockSpec(memory_space=pltpu.SMEM)
VMEM = pl.BlockSpec(memory_space=pltpu.VMEM)
HBM = pl.BlockSpec(memory_space=pltpu.HBM)
ANY = pl.BlockSpec(memory_space=pl.ANY)


def stay(x):
    return pltpu.with_memory_space_constraint(x, pltpu.HBM)


def call(kernel, name, outs, in_specs, out_specs, args, moved=1 << 20, flops=0, scratch=(), aliases={}):
    return pl.pallas_call(
        kernel,
        out_shape=outs,
        in_specs=in_specs,
        out_specs=out_specs,
        scratch_shapes=scratch,
        input_output_aliases=aliases,
        compiler_params=pltpu.CompilerParams(vmem_limit_bytes=VMEM_LIMIT),
        cost_estimate=pl.CostEstimate(flops=16 * moved if moved == LONG else flops, bytes_accessed=moved, transcendentals=0),
        name=name,
    )(*args)


def assign_slots(bl, ln, first_rows, slot_of_list, plan):
    blocks, lists = bl.shape[0], slot_of_list.shape[0]
    for l in range(lists):
        slot_of_list[l] = -1

    def visit(b, nxt, wanted):
        l = bl[b]
        s = slot_of_list[l]
        new = jnp.logical_and(s < 0, wanted)
        slot_of_list[l] = jnp.where(new, nxt, s)
        return nxt + new.astype(i32)

    nxt = jnp.int32(0)
    for b in range(MOVE):
        nxt = visit(b, nxt, True)
    for b in range(MOVE, blocks):
        nxt = visit(b, nxt, ln[b] > first_rows)
    plan[blocks + 1 + MOVE] = nxt
    for b in range(MOVE, blocks):
        nxt = visit(b, nxt, True)
    plan[blocks] = nxt
    for b in range(blocks):
        plan[b] = slot_of_list[bl[b]]


def gram_kernel(bl_hbm, ln_hbm, sources_hbm, points_hbm, targets_hbm, centroids_hbm, table, residual, same, acc, send, *scratch):
    bl, ln, sources, slot_of_list, plan, points, targets, centroids, sems, int_sems = scratch
    blocks, rows, _ = points.shape
    per = acc.shape[0] // CORES
    piece = blocks // PIECES
    copies = [
        pltpu.make_async_copy(bl_hbm, bl, int_sems.at[0]),
        pltpu.make_async_copy(ln_hbm, ln, int_sems.at[1]),
        pltpu.make_async_copy(centroids_hbm, centroids, int_sems.at[2]),
        pltpu.make_async_copy(sources_hbm, sources, int_sems.at[3]),
    ]
    for copy in copies:
        copy.start()
    parts = []
    for i in range(PIECES):
        at = pl.ds(i * piece, piece)
        pair = (
            pltpu.make_async_copy(points_hbm.at[at], points.at[at], sems.at[0, i]),
            pltpu.make_async_copy(targets_hbm.at[at], targets.at[at], sems.at[1, i]),
        )
        for copy in pair:
            copy.start()
        parts.append(pair)
    me = lax.axis_index("narrow")
    core = lax.rem(me, CORES)
    acc[...] = jnp.zeros_like(acc)
    copies[0].wait()
    copies[1].wait()
    assign_slots(bl, ln, CORES * rows, slot_of_list, plan)
    copies[2].wait()
    copies[3].wait()
    for j in range(MOVE):
        plan[blocks + 1 + j] = lax.div(sources[j], blocks)
        mine = lax.rem(plan[j], CORES) == core
        same[j] = jnp.full(same.shape[1:], jnp.where(mine, 1.0, 0.0), f32)
    lanes = lax.broadcasted_iota(i32, table.shape, 1)
    entries = jnp.zeros(table.shape, i32)
    for k in range(plan.shape[0]):
        entries = jnp.where(lanes == k, plan[k], entries)
    table[...] = entries
    row_ids = lax.broadcasted_iota(i32, points.shape[1:], 0) + me * rows
    for i in range(PIECES):
        for copy in parts[i]:
            copy.wait()
        for b in range(i * piece, (i + 1) * piece):
            kept = row_ids < ln[b]
            res = jnp.where(kept, points[b].astype(f32) - centroids[pl.ds(bl[b], 1), :], 0.0).astype(bf16)
            residual[b] = res
            slot = plan[b]
            at = lax.div(slot, CORES) + jnp.where(lax.rem(slot, CORES) == core, 0, per)
            acc[at] += lax.dot_general(res, targets[b], (((0,), (0,)), ((), ())), preferred_element_type=f32)
    for i in range(send.shape[0]):
        send[i] = acc[per + i].astype(bf16)


def lead_sum_kernel(per, acc, recv, chip, *sends):
    at = chip.shape[0]
    chip[...] = (acc[:at] + recv[...].astype(f32)).astype(bf16)
    for out in sends:
        count = out.shape[0]
        out[...] = acc[per + at:per + at + count].astype(bf16)
        at += count


def table_kernel(table, _, out):
    out[...] = table[...]


def sum_kernel(first, acc, recv, *refs):
    out = refs[-1]
    count = out.shape[0]
    out[...] = (acc[first:first + count] + recv[...].astype(f32)).astype(bf16)


def newton_kernel(count, first, offset, extra, keep, acc, recv, *refs):
    pieces, out, chip = refs[:-2], refs[-2], refs[-1]
    grams = []
    for i in range(count):
        g = acc[first + i] + recv[offset + i].astype(f32)
        if keep:
            chip[i] = g
        for which in extra:
            piece, row = which[i]
            g = g + pieces[piece][row].astype(f32)
        grams.append(g)
    polar(grams, out)


def polar(grams, out):
    xs = []
    for g in grams:
        gb = g.astype(bf16)
        p = lax.dot_general(gb, gb, (((1,), (1,)), ((), ())), preferred_element_type=f32)
        scale = lax.rsqrt(jnp.sum(g * g) + 1e-6)
        p = (p * (scale * scale)).astype(bf16)
        xs.append((1.5 * scale) * g - (0.5 * scale) * jnp.dot(p, gb, preferred_element_type=f32))
    for _ in range(ITERS - 1):
        for i, x in enumerate(xs):
            xb = x.astype(bf16)
            p = lax.dot_general(xb, xb, (((1,), (1,)), ((), ())), preferred_element_type=f32).astype(bf16)
            xs[i] = 1.5 * x - 0.5 * jnp.dot(p, xb, preferred_element_type=f32)
    for i, x in enumerate(xs):
        out[i] = x.astype(bf16)


def newton(acc, first, count, recv, offset, crossed, after=(), keep=False, moved=1 << 20):
    extra = [[] for _ in (crossed[0] if crossed else ())]
    flat = []
    for group in crossed:
        for chip, part in enumerate(group):
            extra[chip] += [(len(flat), row) for row in range(part.shape[0])]
            flat.append(part)
    shape = (count,) + acc.shape[1:]
    out = call(
        functools.partial(newton_kernel, count, first, offset, extra, keep),
        "newton",
        (jax.ShapeDtypeStruct(shape, bf16),) + ((jax.ShapeDtypeStruct(shape, f32),) if keep else ()),
        [VMEM] * (2 + len(flat)) + [ANY] * len(after),
        (VMEM,) * (1 + keep),
        (acc, recv, *flat, *after),
        moved=moved,
        scratch=[] if keep else [pltpu.VMEM((8, 128), f32)],
    )
    return out if keep else out[0]


def newton_rest_kernel(others, chip, *refs):
    out = refs[-1]
    grams = []
    for i in range(chip.shape[0]):
        g = chip[i]
        for other in refs[:others]:
            g = g + other[i].astype(f32)
        grams.append(g)
    polar(grams, out)


def leading_kernel(same, residual, own, sibling, out):
    for b in range(MOVE):
        rotation = jnp.where(same[b, :1] > 0.5, own[0], sibling[0])
        out[b] = jnp.dot(residual[b], rotation, preferred_element_type=f32).astype(bf16)


def pair_kernel(near, far, *refs):
    out = refs[-1]
    out[0] = near[...]
    out[1] = far[...]


def arrived_kernel(*refs):
    refs[-1][...] = jnp.zeros_like(refs[-1])


def gather_kernel(starts, n_own, *refs):
    owns, siblings, rots = refs[:n_own], refs[n_own:-1], refs[-1]
    core = lax.rem(lax.axis_index("narrow"), CORES)
    for s, own in zip(starts, owns):
        for i in range(own.shape[0]):
            rots[CORES * (s + i) + core] = own[i]
    for s, sibling in zip(starts, siblings):
        for i in range(sibling.shape[0]):
            rots[CORES * (s + i) + 1 - core] = sibling[i]


def turn_kernel(first, hops, table, residual, main, _, *refs):
    parts = refs[:len(hops)]
    out, rots, turned, sems = refs[-4:]
    blocks, rows, _ = residual.shape
    piece = blocks // STORES
    core = lax.rem(lax.axis_index("narrow"), CORES)
    here = lax.axis_index("wide")
    plan = table[...]
    for i in range(main.shape[0]):
        rots[CORES * (first + i) + 1 - core] = main[i]
    copies = []
    for i in reversed(range(STORES)):
        for b in reversed(range(i * piece, (i + 1) * piece)):
            if b >= MOVE:
                turned[b] = jnp.dot(residual[b], rots[plan[0, b]], preferred_element_type=f32).astype(bf16)
                continue
            donor = plan[0, blocks + 1 + b]
            picked = parts[0][0, b]
            for part, group in zip(parts, hops):
                for k, hop in enumerate(group):
                    match = donor == (hop if len(parts) == 1 else here ^ hop)
                    picked = jnp.where(match, part[k, b], picked)
            turned[b] = picked
        at = pl.ds(i * piece, piece)
        copies.append(pltpu.make_async_copy(turned.at[at], out.at[at], sems.at[i]))
        copies[-1].start()
    for copy in copies:
        copy.wait()


def turn_rest_kernel(first, bl, ln, plan, own, sibling, centroids, points_hbm, _, out, block):
    blocks, rows, _ = points_hbm.shape
    me = lax.axis_index("narrow")
    core = lax.rem(me, CORES)
    row_ids = lax.broadcasted_iota(i32, block.shape, 0) + me * rows

    @pl.loop(MOVE, blocks)
    def _(b):
        @pl.when(plan[b] >= first)
        def _():
            pltpu.sync_copy(points_hbm.at[b], block)
            kept = row_ids < ln[b]
            residual = jnp.where(kept, block[...].astype(f32) - centroids[pl.ds(bl[b], 1), :], 0.0).astype(bf16)
            at = lax.div(plan[b] - first, CORES)
            mine = lax.rem(plan[b], CORES) == core
            rotation = jnp.where(mine, own[at], sibling[at])
            block[...] = jnp.dot(residual, rotation, preferred_element_type=f32).astype(bf16)
            pltpu.sync_copy(block, out.at[b])


def local(wide, narrow, points, targets, centroids, block_list, lengths, sources):
    blocks, rows, width = points.shape
    lists = centroids.shape[0]
    per = lists // CORES
    chips = narrow // CORES
    mat = (width, width)
    lead = MOVE // CORES
    cap = per * 3 // 4 if chips == 2 else per
    rest = per - cap

    entries = blocks + 2 + MOVE
    table, residual, same, acc, send = call(
        gram_kernel,
        "grams",
        (
            jax.ShapeDtypeStruct((8, -(-entries // 128) * 128), i32),
            jax.ShapeDtypeStruct(points.shape, bf16),
            jax.ShapeDtypeStruct((MOVE, 8, width), f32),
            jax.ShapeDtypeStruct((lists,) + mat, f32),
            jax.ShapeDtypeStruct((lead,) + mat, bf16),
        ),
        [HBM] * 6,
        (VMEM,) * 5,
        tuple(stay(x) for x in (block_list, lengths, sources, points, targets, centroids)),
        scratch=[
            pltpu.SMEM((blocks,), i32),
            pltpu.SMEM((blocks,), i32),
            pltpu.SMEM((blocks,), i32),
            pltpu.SMEM((lists,), i32),
            pltpu.SMEM((entries,), i32),
            pltpu.VMEM(points.shape, bf16),
            pltpu.VMEM(points.shape, bf16),
            pltpu.VMEM(centroids.shape, f32),
            pltpu.SemaphoreType.DMA((2, PIECES)),
            pltpu.SemaphoreType.DMA((4,)),
        ],
    )

    to_core = [(i, i ^ 1) for i in range(narrow)]
    to_chip = [[(i, (i + CORES * k) % narrow) for i in range(narrow)] for k in range(1, chips)]

    def cross(part):
        return tuple(lax.ppermute(part, "narrow", perm) for perm in to_chip)

    def swap(part):
        return lax.ppermute(part, "narrow", to_core)

    recv = swap(send)
    counts = (lead, cap - lead) + (rest,) * (rest > 0)
    lead_chip, *sends = call(
        functools.partial(lead_sum_kernel, per),
        "lead_sum",
        tuple(jax.ShapeDtypeStruct((count,) + mat, bf16) for count in counts),
        [VMEM, VMEM],
        (VMEM,) * len(counts),
        (acc, recv),
    )
    lead_crossed = cross(lead_chip)
    recv_main = swap(sends[0])
    after = ()
    if rest:
        late_table = call(
            table_kernel,
            "table",
            jax.ShapeDtypeStruct(table.shape, i32),
            [VMEM, ANY],
            VMEM,
            (table, recv_main),
        )
        overflow = late_table[0, entries - 1] > CORES * cap
        after = (overflow.astype(i32).reshape(1),)
    main_chip = call(
        functools.partial(sum_kernel, lead),
        "main_sum",
        jax.ShapeDtypeStruct((cap - lead,) + mat, bf16),
        [VMEM, VMEM] + [ANY] * len(after),
        VMEM,
        (acc, recv_main, *after),
    )
    main_crossed = cross(main_chip)
    owns = [newton(acc, 0, lead, recv, 0, (lead_crossed,), (main_chip,))]
    siblings = [swap(owns[0])]

    leading = call(
        leading_kernel,
        "turn_leading",
        jax.ShapeDtypeStruct((MOVE, rows, width), bf16),
        [VMEM] * 4,
        VMEM,
        (same, residual, owns[0], siblings[0]),
        flops=LEAD_FLOPS,
    )
    starts, tokens = [0], ()
    if rest:
        starts.append(cap)
        rest_own, rest_chip = newton(acc, cap, rest, swap(sends[1]), 0, (), (leading,), True, 1 << 12)
        owns.append(rest_own)
        tokens = (rest_own,)
    if wide <= 16 and wide & (wide - 1) == 0:
        half = wide // 2
        far = lax.ppermute(leading, "wide", [(i, i ^ half) for i in range(wide)])
        pair = call(
            pair_kernel,
            "pair",
            jax.ShapeDtypeStruct((2,) + leading.shape, bf16),
            [VMEM, VMEM] + [ANY] * len(tokens),
            VMEM,
            (leading, far, *tokens),
            flops=PAIR_FLOPS,
        )
        order = range(half - 1, 0, -1)
        parts = [pair] + [lax.ppermute(pair, "wide", [(i, i ^ k) for i in range(wide)]) for k in order]
        hops = [(k, k ^ half) for k in [0, *order]]
        token = pair
    else:
        parts = [lax.all_gather(leading, "wide", axis=0)]
        hops = [tuple(range(wide))]
        token = leading
    main = newton(acc, lead, cap - lead, recv_main, 0, (main_crossed,), (token,))
    siblings += [swap(own) for own in owns[1:]]
    other = swap(main)

    rots = call(
        functools.partial(gather_kernel, starts + [lead], len(owns) + 1),
        "gather_rotations",
        jax.ShapeDtypeStruct((lists,) + mat, bf16),
        [VMEM] * (1 + len(owns) + len(siblings)),
        VMEM,
        (*owns, main, *siblings),
    )
    token = call(
        arrived_kernel,
        "arrived",
        jax.ShapeDtypeStruct((8, 128), f32),
        [ANY] * (1 + len(parts)),
        VMEM,
        (*parts, rots),
        moved=LONG,
    )
    turned, _ = call(
        functools.partial(turn_kernel, lead, hops),
        "turn",
        (pltpu.HBM(points.shape, bf16), jax.ShapeDtypeStruct(rots.shape, bf16)),
        [VMEM] * (4 + len(parts)) + [ANY],
        (HBM, VMEM),
        (table, residual, other, rots, *parts, token),
        scratch=[
            pltpu.VMEM(points.shape, bf16),
            pltpu.SemaphoreType.DMA((STORES,)),
        ],
        aliases={3: 1},
    )
    if not rest:
        return turned

    def exchange_rest(state):
        turned, chip = state
        own = call(
            functools.partial(newton_rest_kernel, len(to_chip)),
            "newton_rest",
            jax.ShapeDtypeStruct(chip.shape, bf16),
            [VMEM] * (1 + len(to_chip)),
            VMEM,
            (chip, *cross(chip.astype(bf16))),
        )
        turned = call(
            functools.partial(turn_rest_kernel, CORES * cap),
            "turn_rest",
            pltpu.HBM(turned.shape, bf16),
            [SMEM] * 3 + [VMEM] * 3 + [HBM] * 2,
            HBM,
            (block_list, lengths, table[0, :blocks], own, swap(own), centroids, stay(points), stay(turned)),
            scratch=[pltpu.VMEM((rows, width), bf16)],
            aliases={7: 0},
        )
        return turned

    return lax.cond(overflow, exchange_rest, lambda state: state[0], (turned, rest_chip))


def solution(mesh):
    return jax.shard_map(
        functools.partial(local, mesh.shape["wide"], mesh.shape["narrow"]),
        mesh=mesh,
        in_specs=(
            P("wide", "narrow", None),
            P("wide", "narrow", None),
            P("wide", None),
            P("wide"),
            P("wide"),
            P("wide"),
        ),
        out_specs=P("wide", "narrow", None),
        check_vma=False,
    )
```

profile of v0, /device:TPU:0, one launch (start us, length us, event | category | flops | bytes accessed | tf_op | source)
XLA Modules:
  0.0 32.2 jit_solution(5487351069558815510)
XLA Ops:
  0.0 2.9 %grams.1 = (s32[8,128]{1,0:T(8,128)S(1)}, bf16[32,64,256]{2,1,0:T(8,128)(2,1)S(1)}, f32[2,8,256]{2,1,0:T(8,128)S(1)}, f32[16,256,256]{2,1,0:T(8,128)S(1)}, bf16[1,256,256]{2,1,0:T(8,128)(2,1)S(1)}) custom-call(s32[32]{0:T(128)} %bl_hbm.1, s32[32]{0:T(128)} %ln_hbm.1, s32[32]{0:T(128)} %sources_hbm.1, bf16[32,64,256]{2,1,0:T(8,128)(2,1)} %points_hbm.1, ...), custom_call_target="tpu_custom_call" | custom-call | bytes 1048576 | tf_op jit(solution)/shard_map/grams/pallas_call | solution.py:34
  2.9 0.5 %collective-permute-start.2 = (bf16[1,256,256]{2,1,0:T(8,128)(2,1)S(1)}, bf16[1,256,256]{2,1,0:T(8,128)(2,1)S(1)}, u32[]{:S(2)}, u32[]{:S(2)}) collective-permute-start(bf16[1,256,256]{2,1,0:T(8,128)(2,1)S(1)} %get-tuple-element.43), channel_id=1, source_target_pairs={{0,1},{1,0},{2,3},{3,2},{4,5},{5,4},{6,7},{7,6},{8,9},{9,8},{10,11... | collective-permute-start | bytes 393224 | tf_op jit(solution)/shard_map/ppermute | solution.py:331
  3.5 1.0 %collective-permute-done.2.recv = bf16[1,256,256]{2,1,0:T(8,128)(2,1)S(1)} collective-permute-done((bf16[1,256,256]{2,1,0:T(8,128)(2,1)S(1)}, bf16[1,256,256]{2,1,0:T(8,128)(2,1)S(1)}, u32[]{:S(2)}, u32[]{:S(2)}) %collective-permute-start.2) | collective-permute-done | bytes 131104 | tf_op jit(solution)/shard_map/ppermute | solution.py:331
  4.6 0.4 %collective-permute-start.3 = (bf16[5,256,256]{2,1,0:T(8,128)(2,1)S(1)}, bf16[5,256,256]{2,1,0:T(8,128)(2,1)S(1)}, u32[]{:S(2)}, u32[]{:S(2)}) collective-permute-start(bf16[5,256,256]{2,1,0:T(8,128)(2,1)S(1)} %get-tuple-element.44), channel_id=1, source_target_pairs={{0,1},{1,0},{2,3},{3,2},{4,5},{5,4},{6,7},{7,6},{8,9},{9,8},{10,11... | collective-permute-start | bytes 1966088 | tf_op jit(solution)/shard_map/ppermute | solution.py:331
  5.0 2.6 %collective-permute-start.5 = (bf16[1,256,256]{2,1,0:T(8,128)(2,1)S(1)}, bf16[1,256,256]{2,1,0:T(8,128)(2,1)S(1)}, u32[]{:S(2)}, u32[]{:S(2)}) collective-permute-start(bf16[1,256,256]{2,1,0:T(8,128)(2,1)S(1)} %get-tuple-element.47), channel_id=1, source_target_pairs={{0,2},{1,3},{2,0},{3,1},{4,6},{5,7},{6,4},{7,5},{8,10},{9,11},{10,... | collective-permute-start | bytes 393224 | tf_op jit(solution)/shard_map/ppermute | solution.py:328
  7.6 0.6 %slice.6 = s32[1,1]{1,0:T(1,128)} slice(s32[8,128]{1,0:T(8,128)S(1)} %table.1), slice={[0:1], [35:36]} | slice | bytes 8 | tf_op jit(solution)/shard_map/slice | solution.py:355
  8.9 0.1 main_sum.1.refs_1_
  9.0 2.0 %collective-permute-start.4 = (bf16[5,256,256]{2,1,0:T(8,128)(2,1)S(1)}, bf16[5,256,256]{2,1,0:T(8,128)(2,1)S(1)}, u32[]{:S(2)}, u32[]{:S(2)}) collective-permute-start(bf16[5,256,256]{2,1,0:T(8,128)(2,1)S(1)} %main_sum.1.refs_1_), channel_id=1, source_target_pairs={{0,2},{1,3},{2,0},{3,1},{4,6},{5,7},{6,4},{7,5},{8,10},{9,11},{10,... | collective-permute-start | bytes 1966088 | tf_op jit(solution)/shard_map/ppermute | solution.py:328
  11.0 0.6 %collective-permute-done.5.refs_0_ = bf16[1,256,256]{2,1,0:T(8,128)(2,1)S(1)} collective-permute-done((bf16[1,256,256]{2,1,0:T(8,128)(2,1)S(1)}, bf16[1,256,256]{2,1,0:T(8,128)(2,1)S(1)}, u32[]{:S(2)}, u32[]{:S(2)}) %collective-permute-start.5) | collective-permute-done | bytes 131104 | tf_op jit(solution)/shard_map/ppermute | solution.py:328
  11.6 1.6 %newton.3.own.refs_0_ = bf16[1,256,256]{2,1,0:T(8,128)(2,1)S(1)} custom-call(f32[16,256,256]{2,1,0:T(8,128)S(1)} %get-tuple-element.42.acc, bf16[1,256,256]{2,1,0:T(8,128)(2,1)S(1)} %collective-permute-done.2.recv, bf16[1,256,256]{2,1,0:T(8,128)(2,1)S(1)} %collective-permute-done.5.refs_0_, bf16[5,256,256]{2,1,0:T(8,128)(2,1)S(1)} %main_sum.1.refs_1_), custom_call_target="tpu_custom_call" | custom-call | bytes 1048576 | tf_op jit(solution)/shard_map/newton/pallas_call | solution.py:34
  13.4 0.5 %collective-permute-start.8 = (bf16[2,256,256]{2,1,0:T(8,128)(2,1)S(1)}, bf16[2,256,256]{2,1,0:T(8,128)(2,1)S(1)}, u32[]{:S(2)}, u32[]{:S(2)}) collective-permute-start(bf16[2,256,256]{2,1,0:T(8,128)(2,1)S(1)} %get-tuple-element.48), channel_id=1, source_target_pairs={{0,1},{1,0},{2,3},{3,2},{4,5},{5,4},{6,7},{7,6},{8,9},{9,8},{10,11... | collective-permute-start | bytes 786440 | tf_op jit(solution)/shard_map/ppermute | solution.py:331
  13.9 0.8 %collective-permute-done.6.sibling.refs_3_ = bf16[1,256,256]{2,1,0:T(8,128)(2,1)S(1)} collective-permute-done((bf16[1,256,256]{2,1,0:T(8,128)(2,1)S(1)}, bf16[1,256,256]{2,1,0:T(8,128)(2,1)S(1)}, u32[]{:S(2)}, u32[]{:S(2)}) %collective-permute-start.6) | collective-permute-done | bytes 131104 | tf_op jit(solution)/shard_map/ppermute | solution.py:331
  14.7 0.2 turn_leading.1.refs_0_.near
  14.9 2.9 %collective-permute-start.7 = (bf16[2,64,256]{2,1,0:T(8,128)(2,1)S(1)}, bf16[2,64,256]{2,1,0:T(8,128)(2,1)S(1)}, u32[]{:S(2)}, u32[]{:S(2)}) collective-permute-start(bf16[2,64,256]{2,1,0:T(8,128)(2,1)S(1)} %turn_leading.1.refs_0_.near), channel_id=1, source_target_pairs={{0,16},{4,20},{8,24},{12,28},{16,0},{20,4},{24,8},{28,12},{1,17},{... | collective-permute-start | bytes 196616 | tf_op jit(solution)/shard_map/ppermute | solution.py:386
  17.8 1.9 %newton.4 = (bf16[2,256,256]{2,1,0:T(8,128)(2,1)S(1)}, f32[2,256,256]{2,1,0:T(8,128)S(1)}) custom-call(f32[16,256,256]{2,1,0:T(8,128)S(1)} %get-tuple-element.42.acc, bf16[2,256,256]{2,1,0:T(8,128)(2,1)S(1)} %collective-permute-done.8.recv, bf16[2,64,256]{2,1,0:T(8,128)(2,1)S(1)} %turn_leading.1.refs_0_.near), custom_call_target="tpu_custom_call" | custom-call | bytes 4096 | tf_op jit(solution)/shard_map/newton/pallas_call | solution.py:34
  19.8 1.8 %collective-permute-done.7.far = bf16[2,64,256]{2,1,0:T(8,128)(2,1)S(1)} collective-permute-done((bf16[2,64,256]{2,1,0:T(8,128)(2,1)S(1)}, bf16[2,64,256]{2,1,0:T(8,128)(2,1)S(1)}, u32[]{:S(2)}, u32[]{:S(2)}) %collective-permute-start.7) | collective-permute-done | bytes 65568 | tf_op jit(solution)/shard_map/ppermute | solution.py:386
  21.6 1.7 %collective-permute-start.11 = (bf16[2,2,64,256]{3,2,1,0:T(8,128)(2,1)S(1)}, bf16[2,2,64,256]{3,2,1,0:T(8,128)(2,1)S(1)}, u32[]{:S(2)}, u32[]{:S(2)}) collective-permute-start(bf16[2,2,64,256]{3,2,1,0:T(8,128)(2,1)S(1)} %pair.1.refs_1_.refs_0_), channel_id=1, source_target_pairs={{0,12},{4,8},{8,4},{12,0},{16,28},{20,24},{24,20},{28,16},{1,13},{... | collective-permute-start | bytes 393224 | tf_op jit(solution)/shard_map/ppermute | solution.py:397
  23.3 1.5 %collective-permute-start.12 = (bf16[2,2,64,256]{3,2,1,0:T(8,128)(2,1)S(1)}, bf16[2,2,64,256]{3,2,1,0:T(8,128)(2,1)S(1)}, u32[]{:S(2)}, u32[]{:S(2)}) collective-permute-start(bf16[2,2,64,256]{3,2,1,0:T(8,128)(2,1)S(1)} %pair.1.refs_1_.refs_0_), channel_id=1, source_target_pairs={{0,8},{4,12},{8,0},{12,4},{16,24},{20,28},{24,16},{28,20},{1,9},{5... | collective-permute-start | bytes 393224 | tf_op jit(solution)/shard_map/ppermute | solution.py:397
  24.8 0.3 %collective-permute-start.13 = (bf16[2,2,64,256]{3,2,1,0:T(8,128)(2,1)S(1)}, bf16[2,2,64,256]{3,2,1,0:T(8,128)(2,1)S(1)}, u32[]{:S(2)}, u32[]{:S(2)}) collective-permute-start(bf16[2,2,64,256]{3,2,1,0:T(8,128)(2,1)S(1)} %pair.1.refs_1_.refs_0_), channel_id=1, source_target_pairs={{0,4},{4,0},{8,12},{12,8},{16,20},{20,16},{24,28},{28,24},{1,5},{5... | collective-permute-start | bytes 393224 | tf_op jit(solution)/shard_map/ppermute | solution.py:397
  25.2 0.9 %collective-permute-done.4.refs_0_ = bf16[5,256,256]{2,1,0:T(8,128)(2,1)S(1)} collective-permute-done((bf16[5,256,256]{2,1,0:T(8,128)(2,1)S(1)}, bf16[5,256,256]{2,1,0:T(8,128)(2,1)S(1)}, u32[]{:S(2)}, u32[]{:S(2)}) %collective-permute-start.4) | collective-permute-done | bytes 655392 | tf_op jit(solution)/shard_map/ppermute | solution.py:328
  26.0 2.2 %newton.5.refs_2_ = bf16[5,256,256]{2,1,0:T(8,128)(2,1)S(1)} custom-call(f32[16,256,256]{2,1,0:T(8,128)S(1)} %get-tuple-element.42.acc, bf16[5,256,256]{2,1,0:T(8,128)(2,1)S(1)} %collective-permute-done.3._.recv, bf16[5,256,256]{2,1,0:T(8,128)(2,1)S(1)} %collective-permute-done.4.refs_0_, bf16[2,2,64,256]{3,2,1,0:T(8,128)(2,1)S(1)} %pair.1.refs_1_.refs_0_), custom_call_target="tpu_custom_call" | custom-call | bytes 1048576 | tf_op jit(solution)/shard_map/newton/pallas_call | solution.py:34
  28.5 1.4 %collective-permute-done.12.refs_2_ = bf16[2,2,64,256]{3,2,1,0:T(8,128)(2,1)S(1)} collective-permute-done((bf16[2,2,64,256]{3,2,1,0:T(8,128)(2,1)S(1)}, bf16[2,2,64,256]{3,2,1,0:T(8,128)(2,1)S(1)}, u32[]{:S(2)}, u32[]{:S(2)}) %collective-permute-start.12) | collective-permute-done | bytes 131104 | tf_op jit(solution)/shard_map/ppermute | solution.py:397
  29.9 0.6 %collective-permute-done.9.main = bf16[5,256,256]{2,1,0:T(8,128)(2,1)S(1)} collective-permute-done((bf16[5,256,256]{2,1,0:T(8,128)(2,1)S(1)}, bf16[5,256,256]{2,1,0:T(8,128)(2,1)S(1)}, u32[]{:S(2)}, u32[]{:S(2)}) %collective-permute-start.9) | collective-permute-done | bytes 655392 | tf_op jit(solution)/shard_map/ppermute | solution.py:331
  30.5 1.7 %turn.1 = (bf16[32,64,256]{2,1,0:T(8,128)(2,1)}, bf16[16,256,256]{2,1,0:T(8,128)(2,1)S(1)}) custom-call(s32[8,128]{1,0:T(8,128)S(1)} %get-tuple-element.41.table, bf16[32,64,256]{2,1,0:T(8,128)(2,1)S(1)} %get-tuple-element.45.residual, bf16[5,256,256]{2,1,0:T(8,128)(2,1)S(1)} %collective-permute-done.9.main, ...), custom_call_target="tpu_custom_call", output_to_operand_aliasing={{1}: (3, {})} | custom-call | bytes 1048576 | tf_op jit(solution)/shard_map/turn/pallas_call | solution.py:34
  (20 shorter events, 0.5 us)
Async XLA Ops:
  2.9 1.5 %collective-permute-start.2 = (bf16[1,256,256]{2,1,0:T(8,128)(2,1)S(1)}, bf16[1,256,256]{2,1,0:T(8,128)(2,1)S(1)}, u32[]{:S(2)}, u32[]{:S(2)}) collective-permute-start(bf16[1,256,256]{2,1,0:T(8,128)(2,1)S(1)} %get-tuple-element.43), channel_id=1, source_target_pairs={{0,1},{1,0},{2,3},{3,2},{4,5},{5,4},{6,7},{7,6},{8,9},{9,8},{10,11... | collective-permute-start | bytes 393224 | tf_op jit(solution)/shard_map/ppermute | solution.py:331
  4.6 3.1 %collective-permute-start.3 = (bf16[5,256,256]{2,1,0:T(8,128)(2,1)S(1)}, bf16[5,256,256]{2,1,0:T(8,128)(2,1)S(1)}, u32[]{:S(2)}, u32[]{:S(2)}) collective-permute-start(bf16[5,256,256]{2,1,0:T(8,128)(2,1)S(1)} %get-tuple-element.44), channel_id=1, source_target_pairs={{0,1},{1,0},{2,3},{3,2},{4,5},{5,4},{6,7},{7,6},{8,9},{9,8},{10,11... | collective-permute-start | bytes 1966088 | tf_op jit(solution)/shard_map/ppermute | solution.py:331
  5.0 6.7 %collective-permute-start.5 = (bf16[1,256,256]{2,1,0:T(8,128)(2,1)S(1)}, bf16[1,256,256]{2,1,0:T(8,128)(2,1)S(1)}, u32[]{:S(2)}, u32[]{:S(2)}) collective-permute-start(bf16[1,256,256]{2,1,0:T(8,128)(2,1)S(1)} %get-tuple-element.47), channel_id=1, source_target_pairs={{0,2},{1,3},{2,0},{3,1},{4,6},{5,7},{6,4},{7,5},{8,10},{9,11},{10,... | collective-permute-start | bytes 393224 | tf_op jit(solution)/shard_map/ppermute | solution.py:328
  9.0 17.0 %collective-permute-start.4 = (bf16[5,256,256]{2,1,0:T(8,128)(2,1)S(1)}, bf16[5,256,256]{2,1,0:T(8,128)(2,1)S(1)}, u32[]{:S(2)}, u32[]{:S(2)}) collective-permute-start(bf16[5,256,256]{2,1,0:T(8,128)(2,1)S(1)} %main_sum.1.refs_1_), channel_id=1, source_target_pairs={{0,2},{1,3},{2,0},{3,1},{4,6},{5,7},{6,4},{7,5},{8,10},{9,11},{10,... | collective-permute-start | bytes 1966088 | tf_op jit(solution)/shard_map/ppermute | solution.py:328
  13.3 1.4 %collective-permute-start.6 = (bf16[1,256,256]{2,1,0:T(8,128)(2,1)S(1)}, bf16[1,256,256]{2,1,0:T(8,128)(2,1)S(1)}, u32[]{:S(2)}, u32[]{:S(2)}) collective-permute-start(bf16[1,256,256]{2,1,0:T(8,128)(2,1)S(1)} %newton.3.own.refs_0_), channel_id=1, source_target_pairs={{0,1},{1,0},{2,3},{3,2},{4,5},{5,4},{6,7},{7,6},{8,9},{9,8},{10,11... | collective-permute-start | bytes 393224 | tf_op jit(solution)/shard_map/ppermute | solution.py:331
  13.4 4.4 %collective-permute-start.8 = (bf16[2,256,256]{2,1,0:T(8,128)(2,1)S(1)}, bf16[2,256,256]{2,1,0:T(8,128)(2,1)S(1)}, u32[]{:S(2)}, u32[]{:S(2)}) collective-permute-start(bf16[2,256,256]{2,1,0:T(8,128)(2,1)S(1)} %get-tuple-element.48), channel_id=1, source_target_pairs={{0,1},{1,0},{2,3},{3,2},{4,5},{5,4},{6,7},{7,6},{8,9},{9,8},{10,11... | collective-permute-start | bytes 786440 | tf_op jit(solution)/shard_map/ppermute | solution.py:331
  14.9 6.7 %collective-permute-start.7 = (bf16[2,64,256]{2,1,0:T(8,128)(2,1)S(1)}, bf16[2,64,256]{2,1,0:T(8,128)(2,1)S(1)}, u32[]{:S(2)}, u32[]{:S(2)}) collective-permute-start(bf16[2,64,256]{2,1,0:T(8,128)(2,1)S(1)} %turn_leading.1.refs_0_.near), channel_id=1, source_target_pairs={{0,16},{4,20},{8,24},{12,28},{16,0},{20,4},{24,8},{28,12},{1,17},{... | collective-permute-start | bytes 196616 | tf_op jit(solution)/shard_map/ppermute | solution.py:386
  19.7 8.6 %collective-permute-start.10 = (bf16[2,256,256]{2,1,0:T(8,128)(2,1)S(1)}, bf16[2,256,256]{2,1,0:T(8,128)(2,1)S(1)}, u32[]{:S(2)}, u32[]{:S(2)}) collective-permute-start(bf16[2,256,256]{2,1,0:T(8,128)(2,1)S(1)} %get-tuple-element.49.refs_0_.refs_1_), channel_id=1, source_target_pairs={{0,1},{1,0},{2,3},{3,2},{4,5},{5,4},{6,7},{7,6},{8,9},{9,8},{10,11... | collective-permute-start | bytes 786440 | tf_op jit(solution)/shard_map/ppermute | solution.py:331
  21.6 6.9 %collective-permute-start.11 = (bf16[2,2,64,256]{3,2,1,0:T(8,128)(2,1)S(1)}, bf16[2,2,64,256]{3,2,1,0:T(8,128)(2,1)S(1)}, u32[]{:S(2)}, u32[]{:S(2)}) collective-permute-start(bf16[2,2,64,256]{3,2,1,0:T(8,128)(2,1)S(1)} %pair.1.refs_1_.refs_0_), channel_id=1, source_target_pairs={{0,12},{4,8},{8,4},{12,0},{16,28},{20,24},{24,20},{28,16},{1,13},{... | collective-permute-start | bytes 393224 | tf_op jit(solution)/shard_map/ppermute | solution.py:397
  23.3 6.5 %collective-permute-start.12 = (bf16[2,2,64,256]{3,2,1,0:T(8,128)(2,1)S(1)}, bf16[2,2,64,256]{3,2,1,0:T(8,128)(2,1)S(1)}, u32[]{:S(2)}, u32[]{:S(2)}) collective-permute-start(bf16[2,2,64,256]{3,2,1,0:T(8,128)(2,1)S(1)} %pair.1.refs_1_.refs_0_), channel_id=1, source_target_pairs={{0,8},{4,12},{8,0},{12,4},{16,24},{20,28},{24,16},{28,20},{1,9},{5... | collective-permute-start | bytes 393224 | tf_op jit(solution)/shard_map/ppermute | solution.py:397
  24.8 5.0 %collective-permute-start.13 = (bf16[2,2,64,256]{3,2,1,0:T(8,128)(2,1)S(1)}, bf16[2,2,64,256]{3,2,1,0:T(8,128)(2,1)S(1)}, u32[]{:S(2)}, u32[]{:S(2)}) collective-permute-start(bf16[2,2,64,256]{3,2,1,0:T(8,128)(2,1)S(1)} %pair.1.refs_1_.refs_0_), channel_id=1, source_target_pairs={{0,4},{4,0},{8,12},{12,8},{16,20},{20,16},{24,28},{28,24},{1,5},{5... | collective-permute-start | bytes 393224 | tf_op jit(solution)/shard_map/ppermute | solution.py:397
  28.3 2.2 %collective-permute-start.9 = (bf16[5,256,256]{2,1,0:T(8,128)(2,1)S(1)}, bf16[5,256,256]{2,1,0:T(8,128)(2,1)S(1)}, u32[]{:S(2)}, u32[]{:S(2)}) collective-permute-start(bf16[5,256,256]{2,1,0:T(8,128)(2,1)S(1)} %newton.5.refs_2_), channel_id=1, source_target_pairs={{0,1},{1,0},{2,3},{3,2},{4,5},{5,4},{6,7},{7,6},{8,9},{9,8},{10,11... | collective-permute-start | bytes 1966088 | tf_op jit(solution)/shard_map/ppermute | solution.py:331
  29.9 2.3 %copy-start = (f32[16,256]{1,0:T(8,128)S(1)}, f32[16,256]{1,0:T(8,128)}, u32[]{:S(2)}) copy-start(f32[16,256]{1,0:T(8,128)} %centroids_hbm.1) | copy-start | bytes 49156
  29.9 2.3 %copy-start.1 = (s32[32]{0:T(128)S(1)}, s32[32]{0:T(128)}, u32[]{:S(2)}) copy-start(s32[32]{0:T(128)} %bl_hbm.1) | copy-start | bytes 388
  29.9 2.3 %copy-start.2 = (s32[32]{0:T(128)S(1)}, s32[32]{0:T(128)}, u32[]{:S(2)}) copy-start(s32[32]{0:T(128)} %ln_hbm.1) | copy-start | bytes 388
where the time goes:
time: 32.3 us; the launch traced here: 32.2 us
  starting transfers between devices  12.8 us (40%)
  Pallas kernels  10.9 us (34%)
  waiting for transfers between devices  7.07 us (22%)
  between operations  0.79 us (2%)
  local copies, waits for them, and re-layouts  0.6 us (2%)
    pallas_call x12, Pallas kernels, call(): pl.pallas_call(kernel, out_shape=outs, in_specs=in_specs, out_specs=out_s...  10.9 us
    ppermute x2, starting transfers between devices, cross(): return tuple((lax.ppermute(part, 'narrow', perm) for perm in to_chip))  4.65 us
    ppermute x3, starting transfers between devices, local(): lax.ppermute(pair, 'wide', [(i, i ^ k) for i in range(wide)])  3.55 us
    ppermute x1, starting transfers between devices, local(): far = lax.ppermute(leading, 'wide', [(i, i ^ half) for i in range(wide)])  2.91 us
    ppermute x6, waiting for transfers between devices, swap(): return lax.ppermute(part, 'narrow', to_core)  2.39 us
    ppermute x1, waiting for transfers between devices, local(): far = lax.ppermute(leading, 'wide', [(i, i ^ half) for i in range(wide)])  1.8 us
    ppermute x6, starting transfers between devices, swap(): return lax.ppermute(part, 'narrow', to_core)  1.65 us
    ppermute x2, waiting for transfers between devices, cross(): return tuple((lax.ppermute(part, 'narrow', perm) for perm in to_chip))  1.52 us
  transfers between devices with their start and end apart: 12, of which 7 were waited for; matrix products, arithmetic and copies ran while one was open for 2% of the time, Pallas kernels for 19%

commit v1 on v0

--- a/solution.py
+++ b/solution.py
@@ -263,7 +263,7 @@
         copy.wait()
 
 
-def turn_rest_kernel(first, bl, ln, plan, own, sibling, centroids, points_hbm, _, out, block):
+def turn_rest_kernel(first, last, bl, ln, plan, own, sibling, centroids, points_hbm, _, out, block):
     blocks, rows, _ = points_hbm.shape
     me = lax.axis_index("narrow")
     core = lax.rem(me, CORES)
@@ -271,7 +271,7 @@
 
     @pl.loop(MOVE, blocks)
     def _(b):
-        @pl.when(plan[b] >= first)
+        @pl.when(jnp.logical_and(plan[b] >= first, plan[b] < plan[last]))
         def _():
             pltpu.sync_copy(points_hbm.at[b], block)
             kept = row_ids < ln[b]
@@ -449,12 +449,12 @@
             (chip, *cross(chip.astype(bf16))),
         )
         turned = call(
-            functools.partial(turn_rest_kernel, CORES * cap),
+            functools.partial(turn_rest_kernel, CORES * cap, entries - 1),
             "turn_rest",
             pltpu.HBM(turned.shape, bf16),
             [SMEM] * 3 + [VMEM] * 3 + [HBM] * 2,
             HBM,
-            (block_list, lengths, table[0, :blocks], own, swap(own), centroids, stay(points), stay(turned)),
+            (block_list, lengths, table[0, :entries], own, swap(own), centroids, stay(points), stay(turned)),
             scratch=[pltpu.VMEM((rows, width), bf16)],
             aliases={7: 0},
         )

time: 32.3 us -> 32.3 us (level)
  no operation moved by 1% of the time
where the time goes in v1:
time: 32.3 us; the launch traced here: 32.2 us
  starting transfers between devices  12.8 us (40%)
  Pallas kernels  10.9 us (34%)
  waiting for transfers between devices  7.08 us (22%)
  between operations  0.79 us (2%)
  local copies, waits for them, and re-layouts  0.6 us (2%)
    pallas_call x12, Pallas kernels, call(): pl.pallas_call(kernel, out_shape=outs, in_specs=in_specs, out_specs=out_s...  10.9 us
    ppermute x2, starting transfers between devices, cross(): return tuple((lax.ppermute(part, 'narrow', perm) for perm in to_chip))  4.65 us
    ppermute x3, starting transfers between devices, local(): lax.ppermute(pair, 'wide', [(i, i ^ k) for i in range(wide)])  3.55 us
    ppermute x1, starting transfers between devices, local(): far = lax.ppermute(leading, 'wide', [(i, i ^ half) for i in range(wide)])  2.9 us
    ppermute x6, waiting for transfers between devices, swap(): return lax.ppermute(part, 'narrow', to_core)  2.39 us
    ppermute x1, waiting for transfers between devices, local(): far = lax.ppermute(leading, 'wide', [(i, i ^ half) for i in range(wide)])  1.8 us
    ppermute x6, starting transfers between devices, swap(): return lax.ppermute(part, 'narrow', to_core)  1.65 us
    ppermute x2, waiting for transfers between devices, cross(): return tuple((lax.ppermute(part, 'narrow', perm) for perm in to_chip))  1.52 us
  transfers between devices with their start and end apart: 12, of which 7 were waited for; matrix products, arithmetic and copies ran while one was open for 2% of the time, Pallas kernels for 19%

profile of v1, /device:TPU:0, one launch (start us, length us, event | category | flops | bytes accessed | tf_op | source)
XLA Modules:
  0.0 32.2 jit_solution(1103905114370345444)
XLA Ops:
  0.0 2.9 %grams.1 = (s32[8,128]{1,0:T(8,128)S(1)}, bf16[32,64,256]{2,1,0:T(8,128)(2,1)S(1)}, f32[2,8,256]{2,1,0:T(8,128)S(1)}, f32[16,256,256]{2,1,0:T(8,128)S(1)}, bf16[1,256,256]{2,1,0:T(8,128)(2,1)S(1)}) custom-call(s32[32]{0:T(128)} %bl_hbm.1, s32[32]{0:T(128)} %ln_hbm.1, s32[32]{0:T(128)} %sources_hbm.1, bf16[32,64,256]{2,1,0:T(8,128)(2,1)} %points_hbm.1, ...), custom_call_target="tpu_custom_call" | custom-call | bytes 1048576 | tf_op jit(solution)/shard_map/grams/pallas_call | solution.py:34
  2.9 0.5 %collective-permute-start.2 = (bf16[1,256,256]{2,1,0:T(8,128)(2,1)S(1)}, bf16[1,256,256]{2,1,0:T(8,128)(2,1)S(1)}, u32[]{:S(2)}, u32[]{:S(2)}) collective-permute-start(bf16[1,256,256]{2,1,0:T(8,128)(2,1)S(1)} %get-tuple-element.43), channel_id=1, source_target_pairs={{0,1},{1,0},{2,3},{3,2},{4,5},{5,4},{6,7},{7,6},{8,9},{9,8},{10,11... | collective-permute-start | bytes 393224 | tf_op jit(solution)/shard_map/ppermute | solution.py:331
  3.5 1.0 %collective-permute-done.2.recv = bf16[1,256,256]{2,1,0:T(8,128)(2,1)S(1)} collective-permute-done((bf16[1,256,256]{2,1,0:T(8,128)(2,1)S(1)}, bf16[1,256,256]{2,1,0:T(8,128)(2,1)S(1)}, u32[]{:S(2)}, u32[]{:S(2)}) %collective-permute-start.2) | collective-permute-done | bytes 131104 | tf_op jit(solution)/shard_map/ppermute | solution.py:331
  4.5 0.4 %collective-permute-start.3 = (bf16[5,256,256]{2,1,0:T(8,128)(2,1)S(1)}, bf16[5,256,256]{2,1,0:T(8,128)(2,1)S(1)}, u32[]{:S(2)}, u32[]{:S(2)}) collective-permute-start(bf16[5,256,256]{2,1,0:T(8,128)(2,1)S(1)} %get-tuple-element.44), channel_id=1, source_target_pairs={{0,1},{1,0},{2,3},{3,2},{4,5},{5,4},{6,7},{7,6},{8,9},{9,8},{10,11... | collective-permute-start | bytes 1966088 | tf_op jit(solution)/shard_map/ppermute | solution.py:331
  5.0 2.6 %collective-permute-start.5 = (bf16[1,256,256]{2,1,0:T(8,128)(2,1)S(1)}, bf16[1,256,256]{2,1,0:T(8,128)(2,1)S(1)}, u32[]{:S(2)}, u32[]{:S(2)}) collective-permute-start(bf16[1,256,256]{2,1,0:T(8,128)(2,1)S(1)} %get-tuple-element.47), channel_id=1, source_target_pairs={{0,2},{1,3},{2,0},{3,1},{4,6},{5,7},{6,4},{7,5},{8,10},{9,11},{10,... | collective-permute-start | bytes 393224 | tf_op jit(solution)/shard_map/ppermute | solution.py:328
  7.6 0.6 %slice.6 = s32[1,1]{1,0:T(1,128)} slice(s32[8,128]{1,0:T(8,128)S(1)} %table.1), slice={[0:1], [35:36]} | slice | bytes 8 | tf_op jit(solution)/shard_map/slice | solution.py:355
  8.9 0.1 main_sum.1.refs_1_
  9.0 2.0 %collective-permute-start.4 = (bf16[5,256,256]{2,1,0:T(8,128)(2,1)S(1)}, bf16[5,256,256]{2,1,0:T(8,128)(2,1)S(1)}, u32[]{:S(2)}, u32[]{:S(2)}) collective-permute-start(bf16[5,256,256]{2,1,0:T(8,128)(2,1)S(1)} %main_sum.1.refs_1_), channel_id=1, source_target_pairs={{0,2},{1,3},{2,0},{3,1},{4,6},{5,7},{6,4},{7,5},{8,10},{9,11},{10,... | collective-permute-start | bytes 1966088 | tf_op jit(solution)/shard_map/ppermute | solution.py:328
  11.0 0.6 %collective-permute-done.5.refs_0_ = bf16[1,256,256]{2,1,0:T(8,128)(2,1)S(1)} collective-permute-done((bf16[1,256,256]{2,1,0:T(8,128)(2,1)S(1)}, bf16[1,256,256]{2,1,0:T(8,128)(2,1)S(1)}, u32[]{:S(2)}, u32[]{:S(2)}) %collective-permute-start.5) | collective-permute-done | bytes 131104 | tf_op jit(solution)/shard_map/ppermute | solution.py:328
  11.6 1.6 %newton.3.own.refs_0_ = bf16[1,256,256]{2,1,0:T(8,128)(2,1)S(1)} custom-call(f32[16,256,256]{2,1,0:T(8,128)S(1)} %get-tuple-element.42.acc, bf16[1,256,256]{2,1,0:T(8,128)(2,1)S(1)} %collective-permute-done.2.recv, bf16[1,256,256]{2,1,0:T(8,128)(2,1)S(1)} %collective-permute-done.5.refs_0_, bf16[5,256,256]{2,1,0:T(8,128)(2,1)S(1)} %main_sum.1.refs_1_), custom_call_target="tpu_custom_call" | custom-call | bytes 1048576 | tf_op jit(solution)/shard_map/newton/pallas_call | solution.py:34
  13.4 0.5 %collective-permute-start.8 = (bf16[2,256,256]{2,1,0:T(8,128)(2,1)S(1)}, bf16[2,256,256]{2,1,0:T(8,128)(2,1)S(1)}, u32[]{:S(2)}, u32[]{:S(2)}) collective-permute-start(bf16[2,256,256]{2,1,0:T(8,128)(2,1)S(1)} %get-tuple-element.48), channel_id=1, source_target_pairs={{0,1},{1,0},{2,3},{3,2},{4,5},{5,4},{6,7},{7,6},{8,9},{9,8},{10,11... | collective-permute-start | bytes 786440 | tf_op jit(solution)/shard_map/ppermute | solution.py:331
  13.9 0.8 %collective-permute-done.6.sibling.refs_3_ = bf16[1,256,256]{2,1,0:T(8,128)(2,1)S(1)} collective-permute-done((bf16[1,256,256]{2,1,0:T(8,128)(2,1)S(1)}, bf16[1,256,256]{2,1,0:T(8,128)(2,1)S(1)}, u32[]{:S(2)}, u32[]{:S(2)}) %collective-permute-start.6) | collective-permute-done | bytes 131104 | tf_op jit(solution)/shard_map/ppermute | solution.py:331
  14.7 0.2 turn_leading.1.refs_0_.near
  14.9 2.9 %collective-permute-start.7 = (bf16[2,64,256]{2,1,0:T(8,128)(2,1)S(1)}, bf16[2,64,256]{2,1,0:T(8,128)(2,1)S(1)}, u32[]{:S(2)}, u32[]{:S(2)}) collective-permute-start(bf16[2,64,256]{2,1,0:T(8,128)(2,1)S(1)} %turn_leading.1.refs_0_.near), channel_id=1, source_target_pairs={{0,16},{4,20},{8,24},{12,28},{16,0},{20,4},{24,8},{28,12},{1,17},{... | collective-permute-start | bytes 196616 | tf_op jit(solution)/shard_map/ppermute | solution.py:386
  17.8 1.9 %newton.4 = (bf16[2,256,256]{2,1,0:T(8,128)(2,1)S(1)}, f32[2,256,256]{2,1,0:T(8,128)S(1)}) custom-call(f32[16,256,256]{2,1,0:T(8,128)S(1)} %get-tuple-element.42.acc, bf16[2,256,256]{2,1,0:T(8,128)(2,1)S(1)} %collective-permute-done.8.recv, bf16[2,64,256]{2,1,0:T(8,128)(2,1)S(1)} %turn_leading.1.refs_0_.near), custom_call_target="tpu_custom_call" | custom-call | bytes 4096 | tf_op jit(solution)/shard_map/newton/pallas_call | solution.py:34
  19.8 1.8 %collective-permute-done.7.far = bf16[2,64,256]{2,1,0:T(8,128)(2,1)S(1)} collective-permute-done((bf16[2,64,256]{2,1,0:T(8,128)(2,1)S(1)}, bf16[2,64,256]{2,1,0:T(8,128)(2,1)S(1)}, u32[]{:S(2)}, u32[]{:S(2)}) %collective-permute-start.7) | collective-permute-done | bytes 65568 | tf_op jit(solution)/shard_map/ppermute | solution.py:386
  21.6 1.7 %collective-permute-start.11 = (bf16[2,2,64,256]{3,2,1,0:T(8,128)(2,1)S(1)}, bf16[2,2,64,256]{3,2,1,0:T(8,128)(2,1)S(1)}, u32[]{:S(2)}, u32[]{:S(2)}) collective-permute-start(bf16[2,2,64,256]{3,2,1,0:T(8,128)(2,1)S(1)} %pair.1.refs_1_.refs_0_), channel_id=1, source_target_pairs={{0,12},{4,8},{8,4},{12,0},{16,28},{20,24},{24,20},{28,16},{1,13},{... | collective-permute-start | bytes 393224 | tf_op jit(solution)/shard_map/ppermute | solution.py:397
  23.3 1.5 %collective-permute-start.12 = (bf16[2,2,64,256]{3,2,1,0:T(8,128)(2,1)S(1)}, bf16[2,2,64,256]{3,2,1,0:T(8,128)(2,1)S(1)}, u32[]{:S(2)}, u32[]{:S(2)}) collective-permute-start(bf16[2,2,64,256]{3,2,1,0:T(8,128)(2,1)S(1)} %pair.1.refs_1_.refs_0_), channel_id=1, source_target_pairs={{0,8},{4,12},{8,0},{12,4},{16,24},{20,28},{24,16},{28,20},{1,9},{5... | collective-permute-start | bytes 393224 | tf_op jit(solution)/shard_map/ppermute | solution.py:397
  24.8 0.3 %collective-permute-start.13 = (bf16[2,2,64,256]{3,2,1,0:T(8,128)(2,1)S(1)}, bf16[2,2,64,256]{3,2,1,0:T(8,128)(2,1)S(1)}, u32[]{:S(2)}, u32[]{:S(2)}) collective-permute-start(bf16[2,2,64,256]{3,2,1,0:T(8,128)(2,1)S(1)} %pair.1.refs_1_.refs_0_), channel_id=1, source_target_pairs={{0,4},{4,0},{8,12},{12,8},{16,20},{20,16},{24,28},{28,24},{1,5},{5... | collective-permute-start | bytes 393224 | tf_op jit(solution)/shard_map/ppermute | solution.py:397
  25.2 0.9 %collective-permute-done.4.refs_0_ = bf16[5,256,256]{2,1,0:T(8,128)(2,1)S(1)} collective-permute-done((bf16[5,256,256]{2,1,0:T(8,128)(2,1)S(1)}, bf16[5,256,256]{2,1,0:T(8,128)(2,1)S(1)}, u32[]{:S(2)}, u32[]{:S(2)}) %collective-permute-start.4) | collective-permute-done | bytes 655392 | tf_op jit(solution)/shard_map/ppermute | solution.py:328
  26.0 2.3 %newton.5.refs_2_ = bf16[5,256,256]{2,1,0:T(8,128)(2,1)S(1)} custom-call(f32[16,256,256]{2,1,0:T(8,128)S(1)} %get-tuple-element.42.acc, bf16[5,256,256]{2,1,0:T(8,128)(2,1)S(1)} %collective-permute-done.3._.recv, bf16[5,256,256]{2,1,0:T(8,128)(2,1)S(1)} %collective-permute-done.4.refs_0_, bf16[2,2,64,256]{3,2,1,0:T(8,128)(2,1)S(1)} %pair.1.refs_1_.refs_0_), custom_call_target="tpu_custom_call" | custom-call | bytes 1048576 | tf_op jit(solution)/shard_map/newton/pallas_call | solution.py:34
  28.5 1.4 %collective-permute-done.12.refs_2_ = bf16[2,2,64,256]{3,2,1,0:T(8,128)(2,1)S(1)} collective-permute-done((bf16[2,2,64,256]{3,2,1,0:T(8,128)(2,1)S(1)}, bf16[2,2,64,256]{3,2,1,0:T(8,128)(2,1)S(1)}, u32[]{:S(2)}, u32[]{:S(2)}) %collective-permute-start.12) | collective-permute-done | bytes 131104 | tf_op jit(solution)/shard_map/ppermute | solution.py:397
  29.9 0.6 %collective-permute-done.9.main = bf16[5,256,256]{2,1,0:T(8,128)(2,1)S(1)} collective-permute-done((bf16[5,256,256]{2,1,0:T(8,128)(2,1)S(1)}, bf16[5,256,256]{2,1,0:T(8,128)(2,1)S(1)}, u32[]{:S(2)}, u32[]{:S(2)}) %collective-permute-start.9) | collective-permute-done | bytes 655392 | tf_op jit(solution)/shard_map/ppermute | solution.py:331
  30.5 1.7 %turn.1 = (bf16[32,64,256]{2,1,0:T(8,128)(2,1)}, bf16[16,256,256]{2,1,0:T(8,128)(2,1)S(1)}) custom-call(s32[8,128]{1,0:T(8,128)S(1)} %get-tuple-element.41.table, bf16[32,64,256]{2,1,0:T(8,128)(2,1)S(1)} %get-tuple-element.45.residual, bf16[5,256,256]{2,1,0:T(8,128)(2,1)S(1)} %collective-permute-done.9.main, ...), custom_call_target="tpu_custom_call", output_to_operand_aliasing={{1}: (3, {})} | custom-call | bytes 1048576 | tf_op jit(solution)/shard_map/turn/pallas_call | solution.py:34
  (20 shorter events, 0.5 us)
Async XLA Ops:
  2.9 1.5 %collective-permute-start.2 = (bf16[1,256,256]{2,1,0:T(8,128)(2,1)S(1)}, bf16[1,256,256]{2,1,0:T(8,128)(2,1)S(1)}, u32[]{:S(2)}, u32[]{:S(2)}) collective-permute-start(bf16[1,256,256]{2,1,0:T(8,128)(2,1)S(1)} %get-tuple-element.43), channel_id=1, source_target_pairs={{0,1},{1,0},{2,3},{3,2},{4,5},{5,4},{6,7},{7,6},{8,9},{9,8},{10,11... | collective-permute-start | bytes 393224 | tf_op jit(solution)/shard_map/ppermute | solution.py:331
  4.5 3.1 %collective-permute-start.3 = (bf16[5,256,256]{2,1,0:T(8,128)(2,1)S(1)}, bf16[5,256,256]{2,1,0:T(8,128)(2,1)S(1)}, u32[]{:S(2)}, u32[]{:S(2)}) collective-permute-start(bf16[5,256,256]{2,1,0:T(8,128)(2,1)S(1)} %get-tuple-element.44), channel_id=1, source_target_pairs={{0,1},{1,0},{2,3},{3,2},{4,5},{5,4},{6,7},{7,6},{8,9},{9,8},{10,11... | collective-permute-start | bytes 1966088 | tf_op jit(solution)/shard_map/ppermute | solution.py:331
  5.0 6.7 %collective-permute-start.5 = (bf16[1,256,256]{2,1,0:T(8,128)(2,1)S(1)}, bf16[1,256,256]{2,1,0:T(8,128)(2,1)S(1)}, u32[]{:S(2)}, u32[]{:S(2)}) collective-permute-start(bf16[1,256,256]{2,1,0:T(8,128)(2,1)S(1)} %get-tuple-element.47), channel_id=1, source_target_pairs={{0,2},{1,3},{2,0},{3,1},{4,6},{5,7},{6,4},{7,5},{8,10},{9,11},{10,... | collective-permute-start | bytes 393224 | tf_op jit(solution)/shard_map/ppermute | solution.py:328
  9.0 17.0 %collective-permute-start.4 = (bf16[5,256,256]{2,1,0:T(8,128)(2,1)S(1)}, bf16[5,256,256]{2,1,0:T(8,128)(2,1)S(1)}, u32[]{:S(2)}, u32[]{:S(2)}) collective-permute-start(bf16[5,256,256]{2,1,0:T(8,128)(2,1)S(1)} %main_sum.1.refs_1_), channel_id=1, source_target_pairs={{0,2},{1,3},{2,0},{3,1},{4,6},{5,7},{6,4},{7,5},{8,10},{9,11},{10,... | collective-permute-start | bytes 1966088 | tf_op jit(solution)/shard_map/ppermute | solution.py:328
  13.3 1.4 %collective-permute-start.6 = (bf16[1,256,256]{2,1,0:T(8,128)(2,1)S(1)}, bf16[1,256,256]{2,1,0:T(8,128)(2,1)S(1)}, u32[]{:S(2)}, u32[]{:S(2)}) collective-permute-start(bf16[1,256,256]{2,1,0:T(8,128)(2,1)S(1)} %newton.3.own.refs_0_), channel_id=1, source_target_pairs={{0,1},{1,0},{2,3},{3,2},{4,5},{5,4},{6,7},{7,6},{8,9},{9,8},{10,11... | collective-permute-start | bytes 393224 | tf_op jit(solution)/shard_map/ppermute | solution.py:331
  13.4 4.4 %collective-permute-start.8 = (bf16[2,256,256]{2,1,0:T(8,128)(2,1)S(1)}, bf16[2,256,256]{2,1,0:T(8,128)(2,1)S(1)}, u32[]{:S(2)}, u32[]{:S(2)}) collective-permute-start(bf16[2,256,256]{2,1,0:T(8,128)(2,1)S(1)} %get-tuple-element.48), channel_id=1, source_target_pairs={{0,1},{1,0},{2,3},{3,2},{4,5},{5,4},{6,7},{7,6},{8,9},{9,8},{10,11... | collective-permute-start | bytes 786440 | tf_op jit(solution)/shard_map/ppermute | solution.py:331
  14.9 6.7 %collective-permute-start.7 = (bf16[2,64,256]{2,1,0:T(8,128)(2,1)S(1)}, bf16[2,64,256]{2,1,0:T(8,128)(2,1)S(1)}, u32[]{:S(2)}, u32[]{:S(2)}) collective-permute-start(bf16[2,64,256]{2,1,0:T(8,128)(2,1)S(1)} %turn_leading.1.refs_0_.near), channel_id=1, source_target_pairs={{0,16},{4,20},{8,24},{12,28},{16,0},{20,4},{24,8},{28,12},{1,17},{... | collective-permute-start | bytes 196616 | tf_op jit(solution)/shard_map/ppermute | solution.py:386
  19.7 8.7 %collective-permute-start.10 = (bf16[2,256,256]{2,1,0:T(8,128)(2,1)S(1)}, bf16[2,256,256]{2,1,0:T(8,128)(2,1)S(1)}, u32[]{:S(2)}, u32[]{:S(2)}) collective-permute-start(bf16[2,256,256]{2,1,0:T(8,128)(2,1)S(1)} %get-tuple-element.49.refs_0_.refs_1_), channel_id=1, source_target_pairs={{0,1},{1,0},{2,3},{3,2},{4,5},{5,4},{6,7},{7,6},{8,9},{9,8},{10,11... | collective-permute-start | bytes 786440 | tf_op jit(solution)/shard_map/ppermute | solution.py:331
  21.6 6.9 %collective-permute-start.11 = (bf16[2,2,64,256]{3,2,1,0:T(8,128)(2,1)S(1)}, bf16[2,2,64,256]{3,2,1,0:T(8,128)(2,1)S(1)}, u32[]{:S(2)}, u32[]{:S(2)}) collective-permute-start(bf16[2,2,64,256]{3,2,1,0:T(8,128)(2,1)S(1)} %pair.1.refs_1_.refs_0_), channel_id=1, source_target_pairs={{0,12},{4,8},{8,4},{12,0},{16,28},{20,24},{24,20},{28,16},{1,13},{... | collective-permute-start | bytes 393224 | tf_op jit(solution)/shard_map/ppermute | solution.py:397
  23.3 6.5 %collective-permute-start.12 = (bf16[2,2,64,256]{3,2,1,0:T(8,128)(2,1)S(1)}, bf16[2,2,64,256]{3,2,1,0:T(8,128)(2,1)S(1)}, u32[]{:S(2)}, u32[]{:S(2)}) collective-permute-start(bf16[2,2,64,256]{3,2,1,0:T(8,128)(2,1)S(1)} %pair.1.refs_1_.refs_0_), channel_id=1, source_target_pairs={{0,8},{4,12},{8,0},{12,4},{16,24},{20,28},{24,16},{28,20},{1,9},{5... | collective-permute-start | bytes 393224 | tf_op jit(solution)/shard_map/ppermute | solution.py:397
  24.8 5.0 %collective-permute-start.13 = (bf16[2,2,64,256]{3,2,1,0:T(8,128)(2,1)S(1)}, bf16[2,2,64,256]{3,2,1,0:T(8,128)(2,1)S(1)}, u32[]{:S(2)}, u32[]{:S(2)}) collective-permute-start(bf16[2,2,64,256]{3,2,1,0:T(8,128)(2,1)S(1)} %pair.1.refs_1_.refs_0_), channel_id=1, source_target_pairs={{0,4},{4,0},{8,12},{12,8},{16,20},{20,16},{24,28},{28,24},{1,5},{5... | collective-permute-start | bytes 393224 | tf_op jit(solution)/shard_map/ppermute | solution.py:397
  28.3 2.2 %collective-permute-start.9 = (bf16[5,256,256]{2,1,0:T(8,128)(2,1)S(1)}, bf16[5,256,256]{2,1,0:T(8,128)(2,1)S(1)}, u32[]{:S(2)}, u32[]{:S(2)}) collective-permute-start(bf16[5,256,256]{2,1,0:T(8,128)(2,1)S(1)} %newton.5.refs_2_), channel_id=1, source_target_pairs={{0,1},{1,0},{2,3},{3,2},{4,5},{5,4},{6,7},{7,6},{8,9},{9,8},{10,11... | collective-permute-start | bytes 1966088 | tf_op jit(solution)/shard_map/ppermute | solution.py:331
  29.9 2.3 %copy-start = (f32[16,256]{1,0:T(8,128)S(1)}, f32[16,256]{1,0:T(8,128)}, u32[]{:S(2)}) copy-start(f32[16,256]{1,0:T(8,128)} %centroids_hbm.1) | copy-start | bytes 49156
  29.9 2.3 %copy-start.1 = (s32[32]{0:T(128)S(1)}, s32[32]{0:T(128)}, u32[]{:S(2)}) copy-start(s32[32]{0:T(128)} %bl_hbm.1) | copy-start | bytes 388
  29.9 2.3 %copy-start.2 = (s32[32]{0:T(128)S(1)}, s32[32]{0:T(128)}, u32[]{:S(2)}) copy-start(s32[32]{0:T(128)} %ln_hbm.1) | copy-start | bytes 388

commit v2 on v1

--- a/solution.py
+++ b/solution.py
@@ -393,7 +393,7 @@
             (leading, far, *tokens),
             flops=PAIR_FLOPS,
         )
-        order = range(half - 1, 0, -1)
+        order = (half - 1, *range(1, half - 1))
         parts = [pair] + [lax.ppermute(pair, "wide", [(i, i ^ k) for i in range(wide)]) for k in order]
         hops = [(k, k ^ half) for k in [0, *order]]
         token = pair

time: 32.3 us -> 32.3 us (level)
  transfers between devices with their start and end apart: 12 -> 12, of which waited for: 7 -> 8; matrix products, arithmetic and copies ran while one was open for 2% -> 2% of each run, Pallas kernels for 19% -> 19%
where the time goes in v2:
time: 32.3 us; the launch traced here: 32.2 us
  starting transfers between devices  12.8 us (40%)
  Pallas kernels  11 us (34%)
  waiting for transfers between devices  7.08 us (22%)
  between operations  0.78 us (2%)
  local copies, waits for them, and re-layouts  0.6 us (2%)
    pallas_call x12, Pallas kernels, call(): pl.pallas_call(kernel, out_shape=outs, in_specs=in_specs, out_specs=out_s...  11 us
    ppermute x2, starting transfers between devices, cross(): return tuple((lax.ppermute(part, 'narrow', perm) for perm in to_chip))  4.64 us
    ppermute x3, starting transfers between devices, local(): lax.ppermute(pair, 'wide', [(i, i ^ k) for i in range(wide)])  3.55 us
    ppermute x1, starting transfers between devices, local(): far = lax.ppermute(leading, 'wide', [(i, i ^ half) for i in range(wide)])  2.91 us
    ppermute x6, waiting for transfers between devices, swap(): return lax.ppermute(part, 'narrow', to_core)  2.17 us
    ppermute x1, waiting for transfers between devices, local(): far = lax.ppermute(leading, 'wide', [(i, i ^ half) for i in range(wide)])  1.8 us
    ppermute x6, starting transfers between devices, swap(): return lax.ppermute(part, 'narrow', to_core)  1.65 us
    ppermute x3, waiting for transfers between devices, local(): lax.ppermute(pair, 'wide', [(i, i ^ k) for i in range(wide)])  1.61 us
  transfers between devices with their start and end apart: 12, of which 8 were waited for; matrix products, arithmetic and copies ran while one was open for 2% of the time, Pallas kernels for 19%

profile of v2, /device:TPU:0, one launch (start us, length us, event | category | flops | bytes accessed | tf_op | source)
XLA Modules:
  0.0 32.2 jit_solution(10067658124278007952)
XLA Ops:
  0.0 2.9 %grams.1 = (s32[8,128]{1,0:T(8,128)S(1)}, bf16[32,64,256]{2,1,0:T(8,128)(2,1)S(1)}, f32[2,8,256]{2,1,0:T(8,128)S(1)}, f32[16,256,256]{2,1,0:T(8,128)S(1)}, bf16[1,256,256]{2,1,0:T(8,128)(2,1)S(1)}) custom-call(s32[32]{0:T(128)} %bl_hbm.1, s32[32]{0:T(128)} %ln_hbm.1, s32[32]{0:T(128)} %sources_hbm.1, bf16[32,64,256]{2,1,0:T(8,128)(2,1)} %points_hbm.1, ...), custom_call_target="tpu_custom_call" | custom-call | bytes 1048576 | tf_op jit(solution)/shard_map/grams/pallas_call | solution.py:34
  2.9 0.5 %collective-permute-start.2 = (bf16[1,256,256]{2,1,0:T(8,128)(2,1)S(1)}, bf16[1,256,256]{2,1,0:T(8,128)(2,1)S(1)}, u32[]{:S(2)}, u32[]{:S(2)}) collective-permute-start(bf16[1,256,256]{2,1,0:T(8,128)(2,1)S(1)} %get-tuple-element.43), channel_id=1, source_target_pairs={{0,1},{1,0},{2,3},{3,2},{4,5},{5,4},{6,7},{7,6},{8,9},{9,8},{10,11... | collective-permute-start | bytes 393224 | tf_op jit(solution)/shard_map/ppermute | solution.py:331
  3.5 1.0 %collective-permute-done.2.recv = bf16[1,256,256]{2,1,0:T(8,128)(2,1)S(1)} collective-permute-done((bf16[1,256,256]{2,1,0:T(8,128)(2,1)S(1)}, bf16[1,256,256]{2,1,0:T(8,128)(2,1)S(1)}, u32[]{:S(2)}, u32[]{:S(2)}) %collective-permute-start.2) | collective-permute-done | bytes 131104 | tf_op jit(solution)/shard_map/ppermute | solution.py:331
  4.6 0.4 %collective-permute-start.3 = (bf16[5,256,256]{2,1,0:T(8,128)(2,1)S(1)}, bf16[5,256,256]{2,1,0:T(8,128)(2,1)S(1)}, u32[]{:S(2)}, u32[]{:S(2)}) collective-permute-start(bf16[5,256,256]{2,1,0:T(8,128)(2,1)S(1)} %get-tuple-element.44), channel_id=1, source_target_pairs={{0,1},{1,0},{2,3},{3,2},{4,5},{5,4},{6,7},{7,6},{8,9},{9,8},{10,11... | collective-permute-start | bytes 1966088 | tf_op jit(solution)/shard_map/ppermute | solution.py:331
  5.0 2.6 %collective-permute-start.5 = (bf16[1,256,256]{2,1,0:T(8,128)(2,1)S(1)}, bf16[1,256,256]{2,1,0:T(8,128)(2,1)S(1)}, u32[]{:S(2)}, u32[]{:S(2)}) collective-permute-start(bf16[1,256,256]{2,1,0:T(8,128)(2,1)S(1)} %get-tuple-element.47), channel_id=1, source_target_pairs={{0,2},{1,3},{2,0},{3,1},{4,6},{5,7},{6,4},{7,5},{8,10},{9,11},{10,... | collective-permute-start | bytes 393224 | tf_op jit(solution)/shard_map/ppermute | solution.py:328
  7.6 0.6 %slice.6 = s32[1,1]{1,0:T(1,128)} slice(s32[8,128]{1,0:T(8,128)S(1)} %table.1), slice={[0:1], [35:36]} | slice | bytes 8 | tf_op jit(solution)/shard_map/slice | solution.py:355
  9.0 2.0 %collective-permute-start.4 = (bf16[5,256,256]{2,1,0:T(8,128)(2,1)S(1)}, bf16[5,256,256]{2,1,0:T(8,128)(2,1)S(1)}, u32[]{:S(2)}, u32[]{:S(2)}) collective-permute-start(bf16[5,256,256]{2,1,0:T(8,128)(2,1)S(1)} %main_sum.1.refs_1_), channel_id=1, source_target_pairs={{0,2},{1,3},{2,0},{3,1},{4,6},{5,7},{6,4},{7,5},{8,10},{9,11},{10,... | collective-permute-start | bytes 1966088 | tf_op jit(solution)/shard_map/ppermute | solution.py:328
  11.0 0.6 %collective-permute-done.5.refs_0_ = bf16[1,256,256]{2,1,0:T(8,128)(2,1)S(1)} collective-permute-done((bf16[1,256,256]{2,1,0:T(8,128)(2,1)S(1)}, bf16[1,256,256]{2,1,0:T(8,128)(2,1)S(1)}, u32[]{:S(2)}, u32[]{:S(2)}) %collective-permute-start.5) | collective-permute-done | bytes 131104 | tf_op jit(solution)/shard_map/ppermute | solution.py:328
  11.6 1.6 %newton.3.own.refs_0_ = bf16[1,256,256]{2,1,0:T(8,128)(2,1)S(1)} custom-call(f32[16,256,256]{2,1,0:T(8,128)S(1)} %get-tuple-element.42.acc, bf16[1,256,256]{2,1,0:T(8,128)(2,1)S(1)} %collective-permute-done.2.recv, bf16[1,256,256]{2,1,0:T(8,128)(2,1)S(1)} %collective-permute-done.5.refs_0_, bf16[5,256,256]{2,1,0:T(8,128)(2,1)S(1)} %main_sum.1.refs_1_), custom_call_target="tpu_custom_call" | custom-call | bytes 1048576 | tf_op jit(solution)/shard_map/newton/pallas_call | solution.py:34
  13.4 0.5 %collective-permute-start.8 = (bf16[2,256,256]{2,1,0:T(8,128)(2,1)S(1)}, bf16[2,256,256]{2,1,0:T(8,128)(2,1)S(1)}, u32[]{:S(2)}, u32[]{:S(2)}) collective-permute-start(bf16[2,256,256]{2,1,0:T(8,128)(2,1)S(1)} %get-tuple-element.48), channel_id=1, source_target_pairs={{0,1},{1,0},{2,3},{3,2},{4,5},{5,4},{6,7},{7,6},{8,9},{9,8},{10,11... | collective-permute-start | bytes 786440 | tf_op jit(solution)/shard_map/ppermute | solution.py:331
  13.9 0.8 %collective-permute-done.6.sibling.refs_3_ = bf16[1,256,256]{2,1,0:T(8,128)(2,1)S(1)} collective-permute-done((bf16[1,256,256]{2,1,0:T(8,128)(2,1)S(1)}, bf16[1,256,256]{2,1,0:T(8,128)(2,1)S(1)}, u32[]{:S(2)}, u32[]{:S(2)}) %collective-permute-start.6) | collective-permute-done | bytes 131104 | tf_op jit(solution)/shard_map/ppermute | solution.py:331
  14.7 0.2 turn_leading.1.refs_0_.near
  14.9 2.9 %collective-permute-start.7 = (bf16[2,64,256]{2,1,0:T(8,128)(2,1)S(1)}, bf16[2,64,256]{2,1,0:T(8,128)(2,1)S(1)}, u32[]{:S(2)}, u32[]{:S(2)}) collective-permute-start(bf16[2,64,256]{2,1,0:T(8,128)(2,1)S(1)} %turn_leading.1.refs_0_.near), channel_id=1, source_target_pairs={{0,16},{4,20},{8,24},{12,28},{16,0},{20,4},{24,8},{28,12},{1,17},{... | collective-permute-start | bytes 196616 | tf_op jit(solution)/shard_map/ppermute | solution.py:386
  17.8 1.9 %newton.4 = (bf16[2,256,256]{2,1,0:T(8,128)(2,1)S(1)}, f32[2,256,256]{2,1,0:T(8,128)S(1)}) custom-call(f32[16,256,256]{2,1,0:T(8,128)S(1)} %get-tuple-element.42.acc, bf16[2,256,256]{2,1,0:T(8,128)(2,1)S(1)} %collective-permute-done.8.recv, bf16[2,64,256]{2,1,0:T(8,128)(2,1)S(1)} %turn_leading.1.refs_0_.near), custom_call_target="tpu_custom_call" | custom-call | bytes 4096 | tf_op jit(solution)/shard_map/newton/pallas_call | solution.py:34
  19.8 1.8 %collective-permute-done.7.far = bf16[2,64,256]{2,1,0:T(8,128)(2,1)S(1)} collective-permute-done((bf16[2,64,256]{2,1,0:T(8,128)(2,1)S(1)}, bf16[2,64,256]{2,1,0:T(8,128)(2,1)S(1)}, u32[]{:S(2)}, u32[]{:S(2)}) %collective-permute-start.7) | collective-permute-done | bytes 65568 | tf_op jit(solution)/shard_map/ppermute | solution.py:386
  21.6 1.7 %collective-permute-start.11 = (bf16[2,2,64,256]{3,2,1,0:T(8,128)(2,1)S(1)}, bf16[2,2,64,256]{3,2,1,0:T(8,128)(2,1)S(1)}, u32[]{:S(2)}, u32[]{:S(2)}) collective-permute-start(bf16[2,2,64,256]{3,2,1,0:T(8,128)(2,1)S(1)} %pair.1.refs_1_.refs_0_), channel_id=1, source_target_pairs={{0,12},{4,8},{8,4},{12,0},{16,28},{20,24},{24,20},{28,16},{1,13},{... | collective-permute-start | bytes 393224 | tf_op jit(solution)/shard_map/ppermute | solution.py:397
  23.3 0.5 %collective-permute-start.12 = (bf16[2,2,64,256]{3,2,1,0:T(8,128)(2,1)S(1)}, bf16[2,2,64,256]{3,2,1,0:T(8,128)(2,1)S(1)}, u32[]{:S(2)}, u32[]{:S(2)}) collective-permute-start(bf16[2,2,64,256]{3,2,1,0:T(8,128)(2,1)S(1)} %pair.1.refs_1_.refs_0_), channel_id=1, source_target_pairs={{0,4},{4,0},{8,12},{12,8},{16,20},{20,16},{24,28},{28,24},{1,5},{5... | collective-permute-start | bytes 393224 | tf_op jit(solution)/shard_map/ppermute | solution.py:397
  23.9 1.3 %collective-permute-start.13 = (bf16[2,2,64,256]{3,2,1,0:T(8,128)(2,1)S(1)}, bf16[2,2,64,256]{3,2,1,0:T(8,128)(2,1)S(1)}, u32[]{:S(2)}, u32[]{:S(2)}) collective-permute-start(bf16[2,2,64,256]{3,2,1,0:T(8,128)(2,1)S(1)} %pair.1.refs_1_.refs_0_), channel_id=1, source_target_pairs={{0,8},{4,12},{8,0},{12,4},{16,24},{20,28},{24,16},{28,20},{1,9},{5... | collective-permute-start | bytes 393224 | tf_op jit(solution)/shard_map/ppermute | solution.py:397
  25.2 0.9 %collective-permute-done.4.refs_0_ = bf16[5,256,256]{2,1,0:T(8,128)(2,1)S(1)} collective-permute-done((bf16[5,256,256]{2,1,0:T(8,128)(2,1)S(1)}, bf16[5,256,256]{2,1,0:T(8,128)(2,1)S(1)}, u32[]{:S(2)}, u32[]{:S(2)}) %collective-permute-start.4) | collective-permute-done | bytes 655392 | tf_op jit(solution)/shard_map/ppermute | solution.py:328
  26.0 2.3 %newton.5.refs_2_ = bf16[5,256,256]{2,1,0:T(8,128)(2,1)S(1)} custom-call(f32[16,256,256]{2,1,0:T(8,128)S(1)} %get-tuple-element.42.acc, bf16[5,256,256]{2,1,0:T(8,128)(2,1)S(1)} %collective-permute-done.3._.recv, bf16[5,256,256]{2,1,0:T(8,128)(2,1)S(1)} %collective-permute-done.4.refs_0_, bf16[2,2,64,256]{3,2,1,0:T(8,128)(2,1)S(1)} %pair.1.refs_1_.refs_0_), custom_call_target="tpu_custom_call" | custom-call | bytes 1048576 | tf_op jit(solution)/shard_map/newton/pallas_call | solution.py:34
  28.5 1.4 %collective-permute-done.12.refs_2_ = bf16[2,2,64,256]{3,2,1,0:T(8,128)(2,1)S(1)} collective-permute-done((bf16[2,2,64,256]{3,2,1,0:T(8,128)(2,1)S(1)}, bf16[2,2,64,256]{3,2,1,0:T(8,128)(2,1)S(1)}, u32[]{:S(2)}, u32[]{:S(2)}) %collective-permute-start.12) | collective-permute-done | bytes 131104 | tf_op jit(solution)/shard_map/ppermute | solution.py:397
  29.9 0.2 collective-permute-done.13.refs_3_
  30.1 0.3 %collective-permute-done.9.main = bf16[5,256,256]{2,1,0:T(8,128)(2,1)S(1)} collective-permute-done((bf16[5,256,256]{2,1,0:T(8,128)(2,1)S(1)}, bf16[5,256,256]{2,1,0:T(8,128)(2,1)S(1)}, u32[]{:S(2)}, u32[]{:S(2)}) %collective-permute-start.9) | collective-permute-done | bytes 655392 | tf_op jit(solution)/shard_map/ppermute | solution.py:331
  30.5 1.7 %turn.1 = (bf16[32,64,256]{2,1,0:T(8,128)(2,1)}, bf16[16,256,256]{2,1,0:T(8,128)(2,1)S(1)}) custom-call(s32[8,128]{1,0:T(8,128)S(1)} %get-tuple-element.41.table, bf16[32,64,256]{2,1,0:T(8,128)(2,1)S(1)} %get-tuple-element.45.residual, bf16[5,256,256]{2,1,0:T(8,128)(2,1)S(1)} %collective-permute-done.9.main, ...), custom_call_target="tpu_custom_call", output_to_operand_aliasing={{1}: (3, {})} | custom-call | bytes 1048576 | tf_op jit(solution)/shard_map/turn/pallas_call | solution.py:34
  (20 shorter events, 0.6 us)
Async XLA Ops:
  2.9 1.5 %collective-permute-start.2 = (bf16[1,256,256]{2,1,0:T(8,128)(2,1)S(1)}, bf16[1,256,256]{2,1,0:T(8,128)(2,1)S(1)}, u32[]{:S(2)}, u32[]{:S(2)}) collective-permute-start(bf16[1,256,256]{2,1,0:T(8,128)(2,1)S(1)} %get-tuple-element.43), channel_id=1, source_target_pairs={{0,1},{1,0},{2,3},{3,2},{4,5},{5,4},{6,7},{7,6},{8,9},{9,8},{10,11... | collective-permute-start | bytes 393224 | tf_op jit(solution)/shard_map/ppermute | solution.py:331
  4.6 3.1 %collective-permute-start.3 = (bf16[5,256,256]{2,1,0:T(8,128)(2,1)S(1)}, bf16[5,256,256]{2,1,0:T(8,128)(2,1)S(1)}, u32[]{:S(2)}, u32[]{:S(2)}) collective-permute-start(bf16[5,256,256]{2,1,0:T(8,128)(2,1)S(1)} %get-tuple-element.44), channel_id=1, source_target_pairs={{0,1},{1,0},{2,3},{3,2},{4,5},{5,4},{6,7},{7,6},{8,9},{9,8},{10,11... | collective-permute-start | bytes 1966088 | tf_op jit(solution)/shard_map/ppermute | solution.py:331
  5.0 6.7 %collective-permute-start.5 = (bf16[1,256,256]{2,1,0:T(8,128)(2,1)S(1)}, bf16[1,256,256]{2,1,0:T(8,128)(2,1)S(1)}, u32[]{:S(2)}, u32[]{:S(2)}) collective-permute-start(bf16[1,256,256]{2,1,0:T(8,128)(2,1)S(1)} %get-tuple-element.47), channel_id=1, source_target_pairs={{0,2},{1,3},{2,0},{3,1},{4,6},{5,7},{6,4},{7,5},{8,10},{9,11},{10,... | collective-permute-start | bytes 393224 | tf_op jit(solution)/shard_map/ppermute | solution.py:328
  9.0 17.0 %collective-permute-start.4 = (bf16[5,256,256]{2,1,0:T(8,128)(2,1)S(1)}, bf16[5,256,256]{2,1,0:T(8,128)(2,1)S(1)}, u32[]{:S(2)}, u32[]{:S(2)}) collective-permute-start(bf16[5,256,256]{2,1,0:T(8,128)(2,1)S(1)} %main_sum.1.refs_1_), channel_id=1, source_target_pairs={{0,2},{1,3},{2,0},{3,1},{4,6},{5,7},{6,4},{7,5},{8,10},{9,11},{10,... | collective-permute-start | bytes 1966088 | tf_op jit(solution)/shard_map/ppermute | solution.py:328
  13.3 1.4 %collective-permute-start.6 = (bf16[1,256,256]{2,1,0:T(8,128)(2,1)S(1)}, bf16[1,256,256]{2,1,0:T(8,128)(2,1)S(1)}, u32[]{:S(2)}, u32[]{:S(2)}) collective-permute-start(bf16[1,256,256]{2,1,0:T(8,128)(2,1)S(1)} %newton.3.own.refs_0_), channel_id=1, source_target_pairs={{0,1},{1,0},{2,3},{3,2},{4,5},{5,4},{6,7},{7,6},{8,9},{9,8},{10,11... | collective-permute-start | bytes 393224 | tf_op jit(solution)/shard_map/ppermute | solution.py:331
  13.4 4.4 %collective-permute-start.8 = (bf16[2,256,256]{2,1,0:T(8,128)(2,1)S(1)}, bf16[2,256,256]{2,1,0:T(8,128)(2,1)S(1)}, u32[]{:S(2)}, u32[]{:S(2)}) collective-permute-start(bf16[2,256,256]{2,1,0:T(8,128)(2,1)S(1)} %get-tuple-element.48), channel_id=1, source_target_pairs={{0,1},{1,0},{2,3},{3,2},{4,5},{5,4},{6,7},{7,6},{8,9},{9,8},{10,11... | collective-permute-start | bytes 786440 | tf_op jit(solution)/shard_map/ppermute | solution.py:331
  14.9 6.7 %collective-permute-start.7 = (bf16[2,64,256]{2,1,0:T(8,128)(2,1)S(1)}, bf16[2,64,256]{2,1,0:T(8,128)(2,1)S(1)}, u32[]{:S(2)}, u32[]{:S(2)}) collective-permute-start(bf16[2,64,256]{2,1,0:T(8,128)(2,1)S(1)} %turn_leading.1.refs_0_.near), channel_id=1, source_target_pairs={{0,16},{4,20},{8,24},{12,28},{16,0},{20,4},{24,8},{28,12},{1,17},{... | collective-permute-start | bytes 196616 | tf_op jit(solution)/shard_map/ppermute | solution.py:386
  19.7 8.6 %collective-permute-start.10 = (bf16[2,256,256]{2,1,0:T(8,128)(2,1)S(1)}, bf16[2,256,256]{2,1,0:T(8,128)(2,1)S(1)}, u32[]{:S(2)}, u32[]{:S(2)}) collective-permute-start(bf16[2,256,256]{2,1,0:T(8,128)(2,1)S(1)} %get-tuple-element.49.refs_0_.refs_1_), channel_id=1, source_target_pairs={{0,1},{1,0},{2,3},{3,2},{4,5},{5,4},{6,7},{7,6},{8,9},{9,8},{10,11... | collective-permute-start | bytes 786440 | tf_op jit(solution)/shard_map/ppermute | solution.py:331
  21.6 6.9 %collective-permute-start.11 = (bf16[2,2,64,256]{3,2,1,0:T(8,128)(2,1)S(1)}, bf16[2,2,64,256]{3,2,1,0:T(8,128)(2,1)S(1)}, u32[]{:S(2)}, u32[]{:S(2)}) collective-permute-start(bf16[2,2,64,256]{3,2,1,0:T(8,128)(2,1)S(1)} %pair.1.refs_1_.refs_0_), channel_id=1, source_target_pairs={{0,12},{4,8},{8,4},{12,0},{16,28},{20,24},{24,20},{28,16},{1,13},{... | collective-permute-start | bytes 393224 | tf_op jit(solution)/shard_map/ppermute | solution.py:397
  23.3 6.5 %collective-permute-start.12 = (bf16[2,2,64,256]{3,2,1,0:T(8,128)(2,1)S(1)}, bf16[2,2,64,256]{3,2,1,0:T(8,128)(2,1)S(1)}, u32[]{:S(2)}, u32[]{:S(2)}) collective-permute-start(bf16[2,2,64,256]{3,2,1,0:T(8,128)(2,1)S(1)} %pair.1.refs_1_.refs_0_), channel_id=1, source_target_pairs={{0,4},{4,0},{8,12},{12,8},{16,20},{20,16},{24,28},{28,24},{1,5},{5... | collective-permute-start | bytes 393224 | tf_op jit(solution)/shard_map/ppermute | solution.py:397
  23.9 6.2 %collective-permute-start.13 = (bf16[2,2,64,256]{3,2,1,0:T(8,128)(2,1)S(1)}, bf16[2,2,64,256]{3,2,1,0:T(8,128)(2,1)S(1)}, u32[]{:S(2)}, u32[]{:S(2)}) collective-permute-start(bf16[2,2,64,256]{3,2,1,0:T(8,128)(2,1)S(1)} %pair.1.refs_1_.refs_0_), channel_id=1, source_target_pairs={{0,8},{4,12},{8,0},{12,4},{16,24},{20,28},{24,16},{28,20},{1,9},{5... | collective-permute-start | bytes 393224 | tf_op jit(solution)/shard_map/ppermute | solution.py:397
  28.3 2.2 %collective-permute-start.9 = (bf16[5,256,256]{2,1,0:T(8,128)(2,1)S(1)}, bf16[5,256,256]{2,1,0:T(8,128)(2,1)S(1)}, u32[]{:S(2)}, u32[]{:S(2)}) collective-permute-start(bf16[5,256,256]{2,1,0:T(8,128)(2,1)S(1)} %newton.5.refs_2_), channel_id=1, source_target_pairs={{0,1},{1,0},{2,3},{3,2},{4,5},{5,4},{6,7},{7,6},{8,9},{9,8},{10,11... | collective-permute-start | bytes 1966088 | tf_op jit(solution)/shard_map/ppermute | solution.py:331
  30.1 2.0 %copy-start = (f32[16,256]{1,0:T(8,128)S(1)}, f32[16,256]{1,0:T(8,128)}, u32[]{:S(2)}) copy-start(f32[16,256]{1,0:T(8,128)} %centroids_hbm.1) | copy-start | bytes 49156
  30.1 2.0 %copy-start.1 = (s32[32]{0:T(128)S(1)}, s32[32]{0:T(128)}, u32[]{:S(2)}) copy-start(s32[32]{0:T(128)} %bl_hbm.1) | copy-start | bytes 388
  30.1 2.1 %copy-start.2 = (s32[32]{0:T(128)S(1)}, s32[32]{0:T(128)}, u32[]{:S(2)}) copy-start(s32[32]{0:T(128)} %ln_hbm.1) | copy-start | bytes 388

commit v3 on v2

--- a/solution.py
+++ b/solution.py
@@ -15,7 +15,7 @@
 VMEM_LIMIT = 14 * 1024 * 1024
 LONG = 1 << 30
 GROUP = 4
-LEAD_FLOPS = 1350000000
+LEAD_FLOPS = 600000000
 PAIR_FLOPS = 1500000000
 
 f32, bf16, i32 = jnp.float32, jnp.bfloat16, jnp.int32

time: 32.3 us -> 32.3 us (level)
  starting transfers between devices: 12.8 us -> 12.3 us
  waiting for transfers between devices: 7.08 us -> 7.58 us
    ppermute x6, waiting for transfers between devices: 2.17 us -> 2.67 us  [swap(): return lax.ppermute(part, 'narrow', to_core)]
    ppermute x6, starting transfers between devices: 1.65 us -> 1.15 us  [swap(): return lax.ppermute(part, 'narrow', to_core)]
where the time goes in v3:
time: 32.3 us; the launch traced here: 32.2 us
  starting transfers between devices  12.3 us (38%)
  Pallas kernels  11 us (34%)
  waiting for transfers between devices  7.58 us (23%)
  between operations  0.78 us (2%)
  local copies, waits for them, and re-layouts  0.6 us (2%)
    pallas_call x12, Pallas kernels, call(): pl.pallas_call(kernel, out_shape=outs, in_specs=in_specs, out_specs=out_s...  11 us
    ppermute x2, starting transfers between devices, cross(): return tuple((lax.ppermute(part, 'narrow', perm) for perm in to_chip))  4.65 us
    ppermute x3, starting transfers between devices, local(): lax.ppermute(pair, 'wide', [(i, i ^ k) for i in range(wide)])  3.55 us
    ppermute x1, starting transfers between devices, local(): far = lax.ppermute(leading, 'wide', [(i, i ^ half) for i in range(wide)])  2.91 us
    ppermute x6, waiting for transfers between devices, swap(): return lax.ppermute(part, 'narrow', to_core)  2.67 us
    ppermute x1, waiting for transfers between devices, local(): far = lax.ppermute(leading, 'wide', [(i, i ^ half) for i in range(wide)])  1.8 us
    ppermute x3, waiting for transfers between devices, local(): lax.ppermute(pair, 'wide', [(i, i ^ k) for i in range(wide)])  1.6 us
    ppermute x2, waiting for transfers between devices, cross(): return tuple((lax.ppermute(part, 'narrow', perm) for perm in to_chip))  1.51 us
  transfers between devices with their start and end apart: 12, of which 8 were waited for; matrix products, arithmetic and copies ran while one was open for 2% of the time, Pallas kernels for 19%

profile of v3, /device:TPU:0, one launch (start us, length us, event | category | flops | bytes accessed | tf_op | source)
XLA Modules:
  0.0 32.2 jit_solution(3955397447993814388)
XLA Ops:
  0.0 2.9 %grams.1 = (s32[8,128]{1,0:T(8,128)S(1)}, bf16[32,64,256]{2,1,0:T(8,128)(2,1)S(1)}, f32[2,8,256]{2,1,0:T(8,128)S(1)}, f32[16,256,256]{2,1,0:T(8,128)S(1)}, bf16[1,256,256]{2,1,0:T(8,128)(2,1)S(1)}) custom-call(s32[32]{0:T(128)} %bl_hbm.1, s32[32]{0:T(128)} %ln_hbm.1, s32[32]{0:T(128)} %sources_hbm.1, bf16[32,64,256]{2,1,0:T(8,128)(2,1)} %points_hbm.1, ...), custom_call_target="tpu_custom_call" | custom-call | bytes 1048576 | tf_op jit(solution)/shard_map/grams/pallas_call | solution.py:34
  2.9 0.5 %collective-permute-start.2 = (bf16[1,256,256]{2,1,0:T(8,128)(2,1)S(1)}, bf16[1,256,256]{2,1,0:T(8,128)(2,1)S(1)}, u32[]{:S(2)}, u32[]{:S(2)}) collective-permute-start(bf16[1,256,256]{2,1,0:T(8,128)(2,1)S(1)} %get-tuple-element.43), channel_id=1, source_target_pairs={{0,1},{1,0},{2,3},{3,2},{4,5},{5,4},{6,7},{7,6},{8,9},{9,8},{10,11... | collective-permute-start | bytes 393224 | tf_op jit(solution)/shard_map/ppermute | solution.py:331
  3.5 1.0 %collective-permute-done.2.recv = bf16[1,256,256]{2,1,0:T(8,128)(2,1)S(1)} collective-permute-done((bf16[1,256,256]{2,1,0:T(8,128)(2,1)S(1)}, bf16[1,256,256]{2,1,0:T(8,128)(2,1)S(1)}, u32[]{:S(2)}, u32[]{:S(2)}) %collective-permute-start.2) | collective-permute-done | bytes 131104 | tf_op jit(solution)/shard_map/ppermute | solution.py:331
  4.6 0.4 %collective-permute-start.3 = (bf16[5,256,256]{2,1,0:T(8,128)(2,1)S(1)}, bf16[5,256,256]{2,1,0:T(8,128)(2,1)S(1)}, u32[]{:S(2)}, u32[]{:S(2)}) collective-permute-start(bf16[5,256,256]{2,1,0:T(8,128)(2,1)S(1)} %get-tuple-element.44), channel_id=1, source_target_pairs={{0,1},{1,0},{2,3},{3,2},{4,5},{5,4},{6,7},{7,6},{8,9},{9,8},{10,11... | collective-permute-start | bytes 1966088 | tf_op jit(solution)/shard_map/ppermute | solution.py:331
  5.0 2.6 %collective-permute-start.5 = (bf16[1,256,256]{2,1,0:T(8,128)(2,1)S(1)}, bf16[1,256,256]{2,1,0:T(8,128)(2,1)S(1)}, u32[]{:S(2)}, u32[]{:S(2)}) collective-permute-start(bf16[1,256,256]{2,1,0:T(8,128)(2,1)S(1)} %get-tuple-element.47), channel_id=1, source_target_pairs={{0,2},{1,3},{2,0},{3,1},{4,6},{5,7},{6,4},{7,5},{8,10},{9,11},{10,... | collective-permute-start | bytes 393224 | tf_op jit(solution)/shard_map/ppermute | solution.py:328
  7.6 0.6 %slice.6 = s32[1,1]{1,0:T(1,128)} slice(s32[8,128]{1,0:T(8,128)S(1)} %table.1), slice={[0:1], [35:36]} | slice | bytes 8 | tf_op jit(solution)/shard_map/slice | solution.py:355
  8.9 0.1 main_sum.1.refs_1_
  9.0 2.0 %collective-permute-start.4 = (bf16[5,256,256]{2,1,0:T(8,128)(2,1)S(1)}, bf16[5,256,256]{2,1,0:T(8,128)(2,1)S(1)}, u32[]{:S(2)}, u32[]{:S(2)}) collective-permute-start(bf16[5,256,256]{2,1,0:T(8,128)(2,1)S(1)} %main_sum.1.refs_1_), channel_id=1, source_target_pairs={{0,2},{1,3},{2,0},{3,1},{4,6},{5,7},{6,4},{7,5},{8,10},{9,11},{10,... | collective-permute-start | bytes 1966088 | tf_op jit(solution)/shard_map/ppermute | solution.py:328
  11.0 0.6 %collective-permute-done.5.refs_0_ = bf16[1,256,256]{2,1,0:T(8,128)(2,1)S(1)} collective-permute-done((bf16[1,256,256]{2,1,0:T(8,128)(2,1)S(1)}, bf16[1,256,256]{2,1,0:T(8,128)(2,1)S(1)}, u32[]{:S(2)}, u32[]{:S(2)}) %collective-permute-start.5) | collective-permute-done | bytes 131104 | tf_op jit(solution)/shard_map/ppermute | solution.py:328
  11.6 1.6 %newton.3.own.refs_0_ = bf16[1,256,256]{2,1,0:T(8,128)(2,1)S(1)} custom-call(f32[16,256,256]{2,1,0:T(8,128)S(1)} %get-tuple-element.42.acc, bf16[1,256,256]{2,1,0:T(8,128)(2,1)S(1)} %collective-permute-done.2.recv, bf16[1,256,256]{2,1,0:T(8,128)(2,1)S(1)} %collective-permute-done.5.refs_0_, bf16[5,256,256]{2,1,0:T(8,128)(2,1)S(1)} %main_sum.1.refs_1_), custom_call_target="tpu_custom_call" | custom-call | bytes 1048576 | tf_op jit(solution)/shard_map/newton/pallas_call | solution.py:34
  13.4 1.3 %collective-permute-done.6.sibling.refs_3_ = bf16[1,256,256]{2,1,0:T(8,128)(2,1)S(1)} collective-permute-done((bf16[1,256,256]{2,1,0:T(8,128)(2,1)S(1)}, bf16[1,256,256]{2,1,0:T(8,128)(2,1)S(1)}, u32[]{:S(2)}, u32[]{:S(2)}) %collective-permute-start.6) | collective-permute-done | bytes 131104 | tf_op jit(solution)/shard_map/ppermute | solution.py:331
  14.7 0.2 turn_leading.1.refs_0_.near
  14.9 2.9 %collective-permute-start.7 = (bf16[2,64,256]{2,1,0:T(8,128)(2,1)S(1)}, bf16[2,64,256]{2,1,0:T(8,128)(2,1)S(1)}, u32[]{:S(2)}, u32[]{:S(2)}) collective-permute-start(bf16[2,64,256]{2,1,0:T(8,128)(2,1)S(1)} %turn_leading.1.refs_0_.near), channel_id=1, source_target_pairs={{0,16},{4,20},{8,24},{12,28},{16,0},{20,4},{24,8},{28,12},{1,17},{... | collective-permute-start | bytes 196616 | tf_op jit(solution)/shard_map/ppermute | solution.py:386
  17.8 1.9 %newton.4 = (bf16[2,256,256]{2,1,0:T(8,128)(2,1)S(1)}, f32[2,256,256]{2,1,0:T(8,128)S(1)}) custom-call(f32[16,256,256]{2,1,0:T(8,128)S(1)} %get-tuple-element.42.acc, bf16[2,256,256]{2,1,0:T(8,128)(2,1)S(1)} %collective-permute-done.8.recv, bf16[2,64,256]{2,1,0:T(8,128)(2,1)S(1)} %turn_leading.1.refs_0_.near), custom_call_target="tpu_custom_call" | custom-call | bytes 4096 | tf_op jit(solution)/shard_map/newton/pallas_call | solution.py:34
  19.8 1.8 %collective-permute-done.7.far = bf16[2,64,256]{2,1,0:T(8,128)(2,1)S(1)} collective-permute-done((bf16[2,64,256]{2,1,0:T(8,128)(2,1)S(1)}, bf16[2,64,256]{2,1,0:T(8,128)(2,1)S(1)}, u32[]{:S(2)}, u32[]{:S(2)}) %collective-permute-start.7) | collective-permute-done | bytes 65568 | tf_op jit(solution)/shard_map/ppermute | solution.py:386
  21.6 1.7 %collective-permute-start.11 = (bf16[2,2,64,256]{3,2,1,0:T(8,128)(2,1)S(1)}, bf16[2,2,64,256]{3,2,1,0:T(8,128)(2,1)S(1)}, u32[]{:S(2)}, u32[]{:S(2)}) collective-permute-start(bf16[2,2,64,256]{3,2,1,0:T(8,128)(2,1)S(1)} %pair.1.refs_1_.refs_0_), channel_id=1, source_target_pairs={{0,12},{4,8},{8,4},{12,0},{16,28},{20,24},{24,20},{28,16},{1,13},{... | collective-permute-start | bytes 393224 | tf_op jit(solution)/shard_map/ppermute | solution.py:397
  23.3 0.5 %collective-permute-start.12 = (bf16[2,2,64,256]{3,2,1,0:T(8,128)(2,1)S(1)}, bf16[2,2,64,256]{3,2,1,0:T(8,128)(2,1)S(1)}, u32[]{:S(2)}, u32[]{:S(2)}) collective-permute-start(bf16[2,2,64,256]{3,2,1,0:T(8,128)(2,1)S(1)} %pair.1.refs_1_.refs_0_), channel_id=1, source_target_pairs={{0,4},{4,0},{8,12},{12,8},{16,20},{20,16},{24,28},{28,24},{1,5},{5... | collective-permute-start | bytes 393224 | tf_op jit(solution)/shard_map/ppermute | solution.py:397
  23.9 1.3 %collective-permute-start.13 = (bf16[2,2,64,256]{3,2,1,0:T(8,128)(2,1)S(1)}, bf16[2,2,64,256]{3,2,1,0:T(8,128)(2,1)S(1)}, u32[]{:S(2)}, u32[]{:S(2)}) collective-permute-start(bf16[2,2,64,256]{3,2,1,0:T(8,128)(2,1)S(1)} %pair.1.refs_1_.refs_0_), channel_id=1, source_target_pairs={{0,8},{4,12},{8,0},{12,4},{16,24},{20,28},{24,16},{28,20},{1,9},{5... | collective-permute-start | bytes 393224 | tf_op jit(solution)/shard_map/ppermute | solution.py:397
  25.2 0.9 %collective-permute-done.4.refs_0_ = bf16[5,256,256]{2,1,0:T(8,128)(2,1)S(1)} collective-permute-done((bf16[5,256,256]{2,1,0:T(8,128)(2,1)S(1)}, bf16[5,256,256]{2,1,0:T(8,128)(2,1)S(1)}, u32[]{:S(2)}, u32[]{:S(2)}) %collective-permute-start.4) | collective-permute-done | bytes 655392 | tf_op jit(solution)/shard_map/ppermute | solution.py:328
  26.0 2.3 %newton.5.refs_2_ = bf16[5,256,256]{2,1,0:T(8,128)(2,1)S(1)} custom-call(f32[16,256,256]{2,1,0:T(8,128)S(1)} %get-tuple-element.42.acc, bf16[5,256,256]{2,1,0:T(8,128)(2,1)S(1)} %collective-permute-done.3._.recv, bf16[5,256,256]{2,1,0:T(8,128)(2,1)S(1)} %collective-permute-done.4.refs_0_, bf16[2,2,64,256]{3,2,1,0:T(8,128)(2,1)S(1)} %pair.1.refs_1_.refs_0_), custom_call_target="tpu_custom_call" | custom-call | bytes 1048576 | tf_op jit(solution)/shard_map/newton/pallas_call | solution.py:34
  28.5 1.4 %collective-permute-done.12.refs_2_ = bf16[2,2,64,256]{3,2,1,0:T(8,128)(2,1)S(1)} collective-permute-done((bf16[2,2,64,256]{3,2,1,0:T(8,128)(2,1)S(1)}, bf16[2,2,64,256]{3,2,1,0:T(8,128)(2,1)S(1)}, u32[]{:S(2)}, u32[]{:S(2)}) %collective-permute-start.12) | collective-permute-done | bytes 131104 | tf_op jit(solution)/shard_map/ppermute | solution.py:397
  29.9 0.2 collective-permute-done.13.refs_3_
  30.1 0.3 %collective-permute-done.9.main = bf16[5,256,256]{2,1,0:T(8,128)(2,1)S(1)} collective-permute-done((bf16[5,256,256]{2,1,0:T(8,128)(2,1)S(1)}, bf16[5,256,256]{2,1,0:T(8,128)(2,1)S(1)}, u32[]{:S(2)}, u32[]{:S(2)}) %collective-permute-start.9) | collective-permute-done | bytes 655392 | tf_op jit(solution)/shard_map/ppermute | solution.py:331
  30.5 1.7 %turn.1 = (bf16[32,64,256]{2,1,0:T(8,128)(2,1)}, bf16[16,256,256]{2,1,0:T(8,128)(2,1)S(1)}) custom-call(s32[8,128]{1,0:T(8,128)S(1)} %get-tuple-element.41.table, bf16[32,64,256]{2,1,0:T(8,128)(2,1)S(1)} %get-tuple-element.45.residual, bf16[5,256,256]{2,1,0:T(8,128)(2,1)S(1)} %collective-permute-done.9.main, ...), custom_call_target="tpu_custom_call", output_to_operand_aliasing={{1}: (3, {})} | custom-call | bytes 1048576 | tf_op jit(solution)/shard_map/turn/pallas_call | solution.py:34
  (20 shorter events, 0.5 us)
Async XLA Ops:
  2.9 1.5 %collective-permute-start.2 = (bf16[1,256,256]{2,1,0:T(8,128)(2,1)S(1)}, bf16[1,256,256]{2,1,0:T(8,128)(2,1)S(1)}, u32[]{:S(2)}, u32[]{:S(2)}) collective-permute-start(bf16[1,256,256]{2,1,0:T(8,128)(2,1)S(1)} %get-tuple-element.43), channel_id=1, source_target_pairs={{0,1},{1,0},{2,3},{3,2},{4,5},{5,4},{6,7},{7,6},{8,9},{9,8},{10,11... | collective-permute-start | bytes 393224 | tf_op jit(solution)/shard_map/ppermute | solution.py:331
  4.6 3.1 %collective-permute-start.3 = (bf16[5,256,256]{2,1,0:T(8,128)(2,1)S(1)}, bf16[5,256,256]{2,1,0:T(8,128)(2,1)S(1)}, u32[]{:S(2)}, u32[]{:S(2)}) collective-permute-start(bf16[5,256,256]{2,1,0:T(8,128)(2,1)S(1)} %get-tuple-element.44), channel_id=1, source_target_pairs={{0,1},{1,0},{2,3},{3,2},{4,5},{5,4},{6,7},{7,6},{8,9},{9,8},{10,11... | collective-permute-start | bytes 1966088 | tf_op jit(solution)/shard_map/ppermute | solution.py:331
  5.0 6.7 %collective-permute-start.5 = (bf16[1,256,256]{2,1,0:T(8,128)(2,1)S(1)}, bf16[1,256,256]{2,1,0:T(8,128)(2,1)S(1)}, u32[]{:S(2)}, u32[]{:S(2)}) collective-permute-start(bf16[1,256,256]{2,1,0:T(8,128)(2,1)S(1)} %get-tuple-element.47), channel_id=1, source_target_pairs={{0,2},{1,3},{2,0},{3,1},{4,6},{5,7},{6,4},{7,5},{8,10},{9,11},{10,... | collective-permute-start | bytes 393224 | tf_op jit(solution)/shard_map/ppermute | solution.py:328
  9.0 17.0 %collective-permute-start.4 = (bf16[5,256,256]{2,1,0:T(8,128)(2,1)S(1)}, bf16[5,256,256]{2,1,0:T(8,128)(2,1)S(1)}, u32[]{:S(2)}, u32[]{:S(2)}) collective-permute-start(bf16[5,256,256]{2,1,0:T(8,128)(2,1)S(1)} %main_sum.1.refs_1_), channel_id=1, source_target_pairs={{0,2},{1,3},{2,0},{3,1},{4,6},{5,7},{6,4},{7,5},{8,10},{9,11},{10,... | collective-permute-start | bytes 1966088 | tf_op jit(solution)/shard_map/ppermute | solution.py:328
  11.0 6.8 %collective-permute-start.8 = (bf16[2,256,256]{2,1,0:T(8,128)(2,1)S(1)}, bf16[2,256,256]{2,1,0:T(8,128)(2,1)S(1)}, u32[]{:S(2)}, u32[]{:S(2)}) collective-permute-start(bf16[2,256,256]{2,1,0:T(8,128)(2,1)S(1)} %get-tuple-element.48), channel_id=1, source_target_pairs={{0,1},{1,0},{2,3},{3,2},{4,5},{5,4},{6,7},{7,6},{8,9},{9,8},{10,11... | collective-permute-start | bytes 786440 | tf_op jit(solution)/shard_map/ppermute | solution.py:331
  13.3 1.4 %collective-permute-start.6 = (bf16[1,256,256]{2,1,0:T(8,128)(2,1)S(1)}, bf16[1,256,256]{2,1,0:T(8,128)(2,1)S(1)}, u32[]{:S(2)}, u32[]{:S(2)}) collective-permute-start(bf16[1,256,256]{2,1,0:T(8,128)(2,1)S(1)} %newton.3.own.refs_0_), channel_id=1, source_target_pairs={{0,1},{1,0},{2,3},{3,2},{4,5},{5,4},{6,7},{7,6},{8,9},{9,8},{10,11... | collective-permute-start | bytes 393224 | tf_op jit(solution)/shard_map/ppermute | solution.py:331
  14.9 6.7 %collective-permute-start.7 = (bf16[2,64,256]{2,1,0:T(8,128)(2,1)S(1)}, bf16[2,64,256]{2,1,0:T(8,128)(2,1)S(1)}, u32[]{:S(2)}, u32[]{:S(2)}) collective-permute-start(bf16[2,64,256]{2,1,0:T(8,128)(2,1)S(1)} %turn_leading.1.refs_0_.near), channel_id=1, source_target_pairs={{0,16},{4,20},{8,24},{12,28},{16,0},{20,4},{24,8},{28,12},{1,17},{... | collective-permute-start | bytes 196616 | tf_op jit(solution)/shard_map/ppermute | solution.py:386
  19.7 8.6 %collective-permute-start.10 = (bf16[2,256,256]{2,1,0:T(8,128)(2,1)S(1)}, bf16[2,256,256]{2,1,0:T(8,128)(2,1)S(1)}, u32[]{:S(2)}, u32[]{:S(2)}) collective-permute-start(bf16[2,256,256]{2,1,0:T(8,128)(2,1)S(1)} %get-tuple-element.49.refs_0_.refs_1_), channel_id=1, source_target_pairs={{0,1},{1,0},{2,3},{3,2},{4,5},{5,4},{6,7},{7,6},{8,9},{9,8},{10,11... | collective-permute-start | bytes 786440 | tf_op jit(solution)/shard_map/ppermute | solution.py:331
  21.6 6.9 %collective-permute-start.11 = (bf16[2,2,64,256]{3,2,1,0:T(8,128)(2,1)S(1)}, bf16[2,2,64,256]{3,2,1,0:T(8,128)(2,1)S(1)}, u32[]{:S(2)}, u32[]{:S(2)}) collective-permute-start(bf16[2,2,64,256]{3,2,1,0:T(8,128)(2,1)S(1)} %pair.1.refs_1_.refs_0_), channel_id=1, source_target_pairs={{0,12},{4,8},{8,4},{12,0},{16,28},{20,24},{24,20},{28,16},{1,13},{... | collective-permute-start | bytes 393224 | tf_op jit(solution)/shard_map/ppermute | solution.py:397
  23.3 6.5 %collective-permute-start.12 = (bf16[2,2,64,256]{3,2,1,0:T(8,128)(2,1)S(1)}, bf16[2,2,64,256]{3,2,1,0:T(8,128)(2,1)S(1)}, u32[]{:S(2)}, u32[]{:S(2)}) collective-permute-start(bf16[2,2,64,256]{3,2,1,0:T(8,128)(2,1)S(1)} %pair.1.refs_1_.refs_0_), channel_id=1, source_target_pairs={{0,4},{4,0},{8,12},{12,8},{16,20},{20,16},{24,28},{28,24},{1,5},{5... | collective-permute-start | bytes 393224 | tf_op jit(solution)/shard_map/ppermute | solution.py:397
  23.9 6.2 %collective-permute-start.13 = (bf16[2,2,64,256]{3,2,1,0:T(8,128)(2,1)S(1)}, bf16[2,2,64,256]{3,2,1,0:T(8,128)(2,1)S(1)}, u32[]{:S(2)}, u32[]{:S(2)}) collective-permute-start(bf16[2,2,64,256]{3,2,1,0:T(8,128)(2,1)S(1)} %pair.1.refs_1_.refs_0_), channel_id=1, source_target_pairs={{0,8},{4,12},{8,0},{12,4},{16,24},{20,28},{24,16},{28,20},{1,9},{5... | collective-permute-start | bytes 393224 | tf_op jit(solution)/shard_map/ppermute | solution.py:397
  28.3 2.2 %collective-permute-start.9 = (bf16[5,256,256]{2,1,0:T(8,128)(2,1)S(1)}, bf16[5,256,256]{2,1,0:T(8,128)(2,1)S(1)}, u32[]{:S(2)}, u32[]{:S(2)}) collective-permute-start(bf16[5,256,256]{2,1,0:T(8,128)(2,1)S(1)} %newton.5.refs_2_), channel_id=1, source_target_pairs={{0,1},{1,0},{2,3},{3,2},{4,5},{5,4},{6,7},{7,6},{8,9},{9,8},{10,11... | collective-permute-start | bytes 1966088 | tf_op jit(solution)/shard_map/ppermute | solution.py:331
  30.1 2.0 %copy-start = (f32[16,256]{1,0:T(8,128)S(1)}, f32[16,256]{1,0:T(8,128)}, u32[]{:S(2)}) copy-start(f32[16,256]{1,0:T(8,128)} %centroids_hbm.1) | copy-start | bytes 49156
  30.1 2.0 %copy-start.1 = (s32[32]{0:T(128)S(1)}, s32[32]{0:T(128)}, u32[]{:S(2)}) copy-start(s32[32]{0:T(128)} %bl_hbm.1) | copy-start | bytes 388
  30.1 2.1 %copy-start.2 = (s32[32]{0:T(128)S(1)}, s32[32]{0:T(128)}, u32[]{:S(2)}) copy-start(s32[32]{0:T(128)} %ln_hbm.1) | copy-start | bytes 388
